TPU v7x, 32 devices: a whole 2x2x4 slice. The times are simulated.
32 devices in a mesh: rows: 16 (over z, x, core), cols: 2 (over y).
Axes of the slice: x: 2, y: 2, z: 4, core: 2. Of those that a mesh axis runs over, the one named last changes fastest.
Arguments:
- ancestor: bfloat16 [24576, 24576], P('rows', 'cols'), may hold values from -6 to 6
- panel_below: bfloat16 [2048, 512], P('rows'), may hold values from -0.0625 to 0.0625
- panel_beside: bfloat16 [2048, 512], P('rows'), may hold values from -0.0625 to 0.0625
- inverse_lower: bfloat16 [512, 512], replicated, may hold values from -3 to 3
- inverse_upper: bfloat16 [512, 512], replicated, may hold values from -3 to 3
- list_below: int32 [16], replicated, may hold values from 0 to 191, as said below
- list_beside: int32 [16], replicated, may hold values from 0 to 191, as said below
- second_below: bfloat16 [2048, 512], P('rows'), may hold values from -0.0625 to 0.0625
- second_beside: bfloat16 [2048, 512], P('rows'), may hold values from -0.0625 to 0.0625
- linked_below: bfloat16 [512, 512], replicated, may hold values from -0.0625 to 0.0625
- linked_beside: bfloat16 [512, 512], replicated, may hold values from -0.0625 to 0.0625
- second_lower: bfloat16 [512, 512], replicated, may hold values from -3 to 3
- second_upper: bfloat16 [512, 512], replicated, may hold values from -3 to 3
- blocks_below: int32 [16], replicated, may hold values from 0 to 191, as said below
- blocks_beside: int32 [16], replicated, may hold values from 0 to 191, as said below
Outputs:
- new_lower: bfloat16 [24576, 512], P('rows', 'cols')
- new_upper: bfloat16 [24576, 512], P(('cols', 'rows'))
- new_diagonal: bfloat16 [512, 512], P(None, 'cols')
- next_lower: bfloat16 [24576, 512], P('rows', 'cols')
- next_upper: bfloat16 [24576, 512], P(('cols', 'rows'))
- next_link: bfloat16 [512, 512], replicated
- next_diagonal: bfloat16 [512, 512], P(None, 'cols')
Inputs may be any that keep to these rules, and one draw needn't show every extreme that they name: `list_below`: 16 distinct block numbers in ascending order; block 0 and block 191 are always listed. `list_beside`: 16 distinct block numbers in ascending order; block 0 and block 191 are always listed. `blocks_below`: 16 distinct block numbers in ascending order; block 0 and block 191 are always listed. `blocks_beside`: 16 distinct block numbers in ascending order; block 0 and block 191 are always listed.
All inputs are finite; a program needn't handle non-finite values.
Results may differ from a plain program's by a relative error of at most 0.0077.
Values may be sent and summed in bfloat16 or wider, within the bound.
No kernel may reach another device: no remote copies, remote signals or barrier semaphores. Data moves between devices by JAX's collectives and lax.ppermute only.
A program may use at most 256 MiB of HBM per device.

v0:
```python
import jax
import jax.numpy as jnp
from jax import lax
from jax.sharding import PartitionSpec as P

BLK = 128


def normalise(panel, inverse):
    return jnp.dot(panel, inverse, preferred_element_type=jnp.float32).astype(jnp.bfloat16)


def normalise_by_rows(panel, inverse):
    return lax.dot_general(
        panel, inverse, (((1,), (1,)), ((), ())), preferred_element_type=jnp.float32
    ).astype(jnp.bfloat16)


def inner_rows(left, right):
    return lax.dot_general(
        left, right, (((0,), (0,)), ((), ())), preferred_element_type=jnp.float32
    )


def own_half(panel, first_column, half_width):
    return lax.dynamic_slice_in_dim(panel, first_column, half_width, 1)


def listed_columns(tile, blocks, first_block):
    block_count = tile.shape[1] // BLK
    local_ids = blocks - first_block
    inside = jnp.logical_and(local_ids >= 0, local_ids < block_count)
    picked = jnp.take(
        tile.reshape(tile.shape[0], block_count, BLK),
        jnp.clip(local_ids, 0, block_count - 1),
        axis=1,
    )
    return (picked.reshape(tile.shape[0], blocks.shape[0] * BLK), jnp.repeat(inside, BLK))


def masked_product(picked, inside, panel):
    kept = jnp.where(inside[:, None], panel, jnp.zeros_like(panel))
    return jnp.dot(picked, kept, preferred_element_type=jnp.float32)


def listed_rows(strips, blocks):
    shaped = strips.reshape(strips.shape[0] // BLK, BLK, strips.shape[1])
    return jnp.take(shaped, blocks, axis=0).reshape(blocks.shape[0] * BLK, strips.shape[1])


def rows_onto(panel, blocks, first_row, row_count):
    global_rows = first_row + jnp.arange(row_count, dtype=jnp.int32)
    block_of = global_rows // BLK
    offset = global_rows % BLK
    matches = block_of[:, None] == blocks[None, :]
    position = jnp.sum(
        jnp.where(matches, jnp.arange(blocks.shape[0], dtype=jnp.int32)[None, :], 0), axis=1
    )
    present = jnp.any(matches, axis=1)
    picked = jnp.take(panel, position * BLK + offset, axis=0)
    return jnp.where(present[:, None], picked, jnp.zeros_like(picked))


def lower_block(partial_value):
    return (-lax.psum_scatter(partial_value, "cols", scatter_dimension=1, tiled=True)).astype(
        jnp.bfloat16
    )


def diag_block(base_value, picked_rows, lower_local):
    summed = lax.psum(inner_rows(picked_rows, lower_local), "rows")
    return (base_value - summed).astype(jnp.bfloat16)


def body(
    ancestor,
    panel_below,
    panel_beside,
    inverse_lower,
    inverse_upper,
    list_below,
    list_beside,
    second_below,
    second_beside,
    linked_below,
    linked_beside,
    second_lower,
    second_upper,
    blocks_below,
    blocks_beside,
):
    row_devices = lax.axis_size("rows")
    row_at = lax.axis_index("rows")
    col_at = lax.axis_index("cols")
    col_devices = lax.axis_size("cols")
    tile_rows = ancestor.shape[0]
    tile_cols = ancestor.shape[1]
    width = inverse_lower.shape[0]
    half_width = width // col_devices
    first_column = col_at * half_width
    unit_below = normalise(panel_below, inverse_lower)
    unit_beside = normalise_by_rows(panel_beside, inverse_upper)
    below_next = normalise(second_below, second_lower)
    beside_next = normalise_by_rows(second_beside, second_upper)
    unit_below, unit_beside, below_next, beside_next = (
        lax.all_gather(unit_below, "rows", axis=0, tiled=True),
        lax.all_gather(unit_beside, "rows", axis=0, tiled=True),
        lax.all_gather(below_next, "rows", axis=0, tiled=True),
        lax.all_gather(beside_next, "rows", axis=0, tiled=True),
    )
    strips = lax.all_to_all(ancestor, "rows", split_axis=1, concat_axis=0, tiled=True)
    strip_width = tile_cols // row_devices
    strip_start = (col_at * row_devices + row_at) * strip_width
    first_block = col_at * (tile_cols // BLK)
    row_start = row_at * tile_rows
    picked, inside = listed_columns(ancestor, list_below, first_block)
    new_lower = lower_block(masked_product(picked, inside, unit_below))
    new_upper = (-inner_rows(listed_rows(strips, list_beside), unit_beside)).astype(jnp.bfloat16)
    base_first = jnp.dot(
        inverse_upper,
        own_half(inverse_lower, first_column, half_width),
        preferred_element_type=jnp.float32,
    )
    new_diagonal = diag_block(
        base_first, rows_onto(unit_beside, list_beside, row_start, tile_rows), new_lower
    )
    link_below = normalise(linked_below, second_lower)
    link_beside = normalise_by_rows(linked_beside, second_upper)
    link_rows = lax.dynamic_slice_in_dim(link_below, first_column, half_width, 0)
    picked_next, inside_next = listed_columns(ancestor, blocks_below, first_block)
    partial_value = masked_product(picked_next, inside_next, below_next) + jnp.dot(
        new_lower, link_rows, preferred_element_type=jnp.float32
    )
    next_lower = lower_block(partial_value)
    first_row = (row_at == 0).astype(jnp.float32)
    link_term = inner_rows(
        new_upper, rows_onto(below_next, blocks_below, strip_start, strip_width)
    ) + first_row * jnp.dot(new_diagonal, link_rows, preferred_element_type=jnp.float32)
    next_link = (-lax.psum(link_term, ("rows", "cols"))).astype(jnp.bfloat16)
    next_upper = (
        -(
            inner_rows(listed_rows(strips, blocks_beside), beside_next)
            + jnp.dot(new_upper, link_beside, preferred_element_type=jnp.float32)
        )
    ).astype(jnp.bfloat16)
    base_second = jnp.dot(
        second_upper,
        own_half(second_lower, first_column, half_width),
        preferred_element_type=jnp.float32,
    ) - inner_rows(link_beside, own_half(next_link, first_column, half_width))
    next_diagonal = diag_block(
        base_second, rows_onto(beside_next, blocks_beside, row_start, tile_rows), next_lower
    )
    return (new_lower, new_upper, new_diagonal, next_lower, next_upper, next_link, next_diagonal)


def solution(mesh):
    return jax.shard_map(
        body,
        mesh=mesh,
        in_specs=(
            P("rows", "cols"),
            P("rows", None),
            P("rows", None),
            P(),
            P(),
            P(),
            P(),
            P("rows", None),
            P("rows", None),
            P(),
            P(),
            P(),
            P(),
            P(),
            P(),
        ),
        out_specs=(
            P("rows", "cols"),
            P(("cols", "rows"), None),
            P(None, "cols"),
            P("rows", "cols"),
            P(("cols", "rows"), None),
            P(),
            P(None, "cols"),
        ),
        check_vma=False,
    )
```

profile of v0, /device:TPU:0, one launch (start us, length us, event | category | flops | bytes accessed | tf_op | source)
XLA Modules:
  0.0 1304.3 jit_solution(1387711838850980001)
XLA Ops:
  7.2 48.8 %copy.44 = bf16[1536,12288]{0,1:T(8,128)(2,1)} copy(bf16[1536,12288]{1,0:T(8,128)(2,1)} %param.21) | data formatting | bytes 75497472 | tf_op args[0]
  56.0 7.5 all-to-all-start
  65.6 43.8 %copy.45 = bf16[1536,96,128]{2,0,1:T(8,128)(2,1)} copy(bf16[1536,96,128]{0,2,1:T(8,128)(2,1)} %bitcast.59) | data formatting | bytes 75497472 | tf_op jit(solution)/shard_map/reshape | solution.py:34
  109.4 6.9 gather_fusion.1
  116.3 6.1 select_bitcast_fusion.1
  122.4 8.6 copy.46
  131.1 457.8 %all-gather.5.cloned.1.call-done = bf16[2048,512]{1,0:T(8,128)(2,1)} async-done(((bf16[128,512]{1,0:T(8,128)(2,1)}), bf16[2048,512]{1,0:T(8,128)(2,1)}) %all-gather.5.cloned.1.call-update) | async-done | bytes 2097168 | tf_op jit(solution)/shard_map/all_gather | solution.py:106
  588.9 8.6 fusion.2
  600.9 6.8 gather_fusion.4
  607.7 6.0 select_bitcast_fusion
  613.7 8.7 copy.51
  622.9 94.7 %all-gather.9.cloned.1.call-done = bf16[2048,512]{1,0:T(8,128)(2,1)} async-done(((bf16[128,512]{1,0:T(8,128)(2,1)}), bf16[2048,512]{1,0:T(8,128)(2,1)}) %all-gather.9.cloned.1.call-update) | async-done | bytes 2097168 | tf_op jit(solution)/shard_map/all_gather | solution.py:108
  717.6 8.6 fusion
  726.2 35.7 %reduce-scatter.3.cloned.1.call-done = f32[1536,256]{1,0:T(8,128)} async-done(((f32[1536,512]{1,0:T(8,128)}), f32[1536,256]{1,0:T(8,128)}) %reduce-scatter.3.cloned.1.call-update) | async-done | bytes 1572880 | tf_op jit(solution)/shard_map/reduce_scatter | solution.py:65
  763.5 4.4 convolution_add_fusion
  769.0 56.7 %all-gather.11.cloned.1.call-done = bf16[2048,512]{1,0:T(8,128)(2,1)} async-done(((bf16[128,512]{1,0:T(8,128)(2,1)}), bf16[2048,512]{1,0:T(8,128)(2,1)}) %all-gather.11.cloned.1.call-update) | async-done | bytes 2097168 | tf_op jit(solution)/shard_map/all_gather | solution.py:109
  825.7 7.4 gather_fusion.6
  833.1 124.7 %all-gather.7.cloned.1.call-done = bf16[2048,512]{1,0:T(8,128)(2,1)} async-done(((bf16[128,512]{1,0:T(8,128)(2,1)}), bf16[2048,512]{1,0:T(8,128)(2,1)}) %all-gather.7.cloned.1.call-update) | async-done | bytes 2097168 | tf_op jit(solution)/shard_map/all_gather | solution.py:107
  957.7 6.7 gather_fusion.3
  966.2 35.8 %reduce-scatter.5.cloned.1.call-done = f32[1536,256]{1,0:T(8,128)} async-done(((f32[1536,512]{1,0:T(8,128)}), f32[1536,256]{1,0:T(8,128)}) %reduce-scatter.5.cloned.1.call-update) | async-done | bytes 1572880 | tf_op jit(solution)/shard_map/reduce_scatter | solution.py:65
  1013.1 88.1 %all-reduce.6.cloned.1.call-done = (f32[512,256]{0,1:T(8,128)}, f32[512,256]{0,1:T(8,128)}) async-done(((f32[512,256]{0,1:T(8,128)}, f32[512,256]{0,1:T(8,128)}), (f32[512,256]{0,1:T(8,128)}, f32[512,256]{0,1:T(8,128)})) %all-reduce.6.cloned.1.call-update) | async-done | bytes 1048592 | tf_op jit(solution)/shard_map/psum | solution.py:71
  1105.0 48.7 %copy.48 = bf16[16,1536,768]{2,1,0:T(8,128)(2,1)} copy(bf16[16,1536,768]{1,2,0:T(8,128)(2,1)} %bitcast.5) | data formatting | bytes 75497472 | tf_op jit(solution)/shard_map/all_to_all | solution.py:111
  1164.2 4.3 gather_fusion.5
  1174.4 119.1 %all-reduce.4.cloned.1.call-done = f32[512,512]{1,0:T(8,128)} async-done(((f32[512,512]{1,0:T(8,128)}), f32[512,512]{1,0:T(8,128)}) %all-reduce.4.cloned.1.call-update) | async-done | bytes 1048592 | tf_op jit(solution)/shard_map/psum | solution.py:139
  (111 shorter events, 45.1 us)
Async XLA Ops:
  7.2 57.4 %copy-start = (bf16[512,512]{1,0:T(8,128)(2,1)S(1)}, bf16[512,512]{1,0:T(8,128)(2,1)}, u32[]{:S(2)}) copy-start(bf16[512,512]{1,0:T(8,128)(2,1)} %param.32) | copy-start | bytes 1572868
  55.9 7.6 copy-start.10
  56.0 7.6 copy-start.15
  56.0 8.6 copy-start.16
  56.0 1049.0 %all-to-all-start = ((bf16[1536,16,768]{0,2,1:T(8,128)(2,1)}), bf16[1536,16,768]{0,2,1:T(8,128)(2,1)}, u32[]{:S(2)}, u32[]{:S(2)}) async-start(bf16[1536,16,768]{0,2,1:T(8,128)(2,1)} %bitcast.58), calls=%async_computation.1 | async-start | bytes 75497472 | tf_op jit(solution)/shard_map/all_to_all | solution.py:111
  63.5 525.4 %all-gather.5.cloned.1.call-start = ((), (), s32[]{:S(2)}) async-start(), calls=%async_computation.3 | async-start | bytes 2228224 | tf_op jit(solution)/shard_map/all_gather | solution.py:106
  64.5 653.1 %all-gather.9.cloned.1.call-start = ((), (), s32[]{:S(2)}) async-start(), calls=%async_computation.6 | async-start | bytes 2228224 | tf_op jit(solution)/shard_map/all_gather | solution.py:108
  65.5 696.4 %reduce-scatter.3.cloned.1.call-start = ((), (), s32[]{:S(2)}) async-start(), calls=%async_computation.4 | async-start | bytes 4718592 | tf_op jit(solution)/shard_map/reduce_scatter | solution.py:65
  65.5 43.8 %copy-start.21 = (s32[16]{0:T(128)S(1)}, s32[16]{0:T(128)}, u32[]{:S(2)}) copy-start(s32[16]{0:T(128)} %param.34) | copy-start | bytes 196
  65.5 43.8 %copy-start.22 = (s32[16]{0:T(128)S(1)}, s32[16]{0:T(128)}, u32[]{:S(2)}) copy-start(s32[16]{0:T(128)} %param.26) | copy-start | bytes 196
  597.6 228.1 %all-gather.11.cloned.1.call-start = ((), (), s32[]{:S(2)}) async-start(), calls=%async_computation.8 | async-start | bytes 2228224 | tf_op jit(solution)/shard_map/all_gather | solution.py:109
  599.6 358.2 %all-gather.7.cloned.1.call-start = ((), (), s32[]{:S(2)}) async-start(), calls=%async_computation.5 | async-start | bytes 2228224 | tf_op jit(solution)/shard_map/all_gather | solution.py:107
  600.6 401.4 %reduce-scatter.5.cloned.1.call-start = ((), (), s32[]{:S(2)}) async-start(), calls=%async_computation.7 | async-start | bytes 4718592 | tf_op jit(solution)/shard_map/reduce_scatter | solution.py:65
  613.7 8.7 copy-start.14
  622.9 140.6 %copy-start.8 = (bf16[512,512]{1,0:T(8,128)(2,1)}, bf16[512,512]{1,0:T(8,128)(2,1)S(1)}, u32[]{:S(2)}) copy-start(bf16[512,512]{1,0:T(8,128)(2,1)S(1)} %fusion.63) | copy-start | bytes 1572868
  763.5 201.0 %copy-start.6 = (bf16[1536,256]{1,0:T(8,128)(2,1)}, bf16[1536,256]{1,0:T(8,128)(2,1)S(1)}, u32[]{:S(2)}) copy-start(bf16[1536,256]{1,0:T(8,128)(2,1)S(1)} %negate_convert_fusion.3) | copy-start | bytes 2359300
  767.9 333.3 %all-reduce.6.cloned.1.call-start = ((), (), s32[]{:S(2)}) async-start(), calls=%async_computation.10 | async-start | bytes 2097152 | tf_op jit(solution)/shard_map/psum | solution.py:71
  1004.5 5.3 copy-start.3
  1007.8 285.7 %all-reduce.4.cloned.1.call-start = ((), (), s32[]{:S(2)}) async-start(), calls=%async_computation.9 | async-start | bytes 2097152 | tf_op jit(solution)/shard_map/psum | solution.py:139
  1158.0 2.5 copy-start.2
  1162.4 10.5 copy-start.11
  1168.5 2.6 copy-start.1
  1172.9 122.3 %copy-start.5 = (bf16[512,512]{1,0:T(8,128)(2,1)S(1)}, bf16[512,512]{1,0:T(8,128)(2,1)}, u32[]{:S(2)}) copy-start(bf16[512,512]{1,0:T(8,128)(2,1)} %param.33) | copy-start | bytes 1572868
  1294.9 2.6 copy-start.9
  (8 other events, 10.3 us)
Sparse Core Ops, SparseCore 0:
  67.1 521.8 all-gather.4
  591.7 125.9 all-gather.8
  719.9 41.9 reduce-scatter.2
  764.7 60.9 all-gather.10
  828.5 129.1 all-gather.6
  959.9 42.0 reduce-scatter.4
  1007.9 93.2 all-reduce.5
  1164.3 129.1 all-reduce.3
where the time goes:
time: 1310 us; the launch traced here: 1300 us
  waiting for transfers between devices  1010 us (77%)
  local copies, waits for them, and re-layouts  203 us (15%)
  matrix products  43.9 us (3%)
  other arithmetic  22 us (2%)
  between operations  14.6 us (1%)
    all_gather x1, waiting for transfers between devices, body(): lax.all_gather(unit_below, 'rows', axis=0, tiled=True)  458 us
    all_gather x1, waiting for transfers between devices, body(): lax.all_gather(unit_beside, 'rows', axis=0, tiled=True)  125 us
    psum x1, waiting for transfers between devices, body(): next_link = (-lax.psum(link_term, ('rows', 'cols'))).astype(jnp.bfloat16)  119 us
    all_gather x1, waiting for transfers between devices, body(): lax.all_gather(below_next, 'rows', axis=0, tiled=True)  94.7 us
    psum x1, waiting for transfers between devices, diag_block(): summed = lax.psum(inner_rows(picked_rows, lower_local), 'rows')  88.1 us
    reduce_scatter x2, waiting for transfers between devices, lower_block(): lax.psum_scatter(partial_value, 'cols', scatter_dimension=1, tiled=True)  71.5 us
    all_gather x1, waiting for transfers between devices, body(): lax.all_gather(beside_next, 'rows', axis=0, tiled=True)  56.7 us
    unnamed x49, local copies, waits for them, and re-layouts  53.1 us
  transfers between devices with their start and end apart: 9, of which 8 were waited for; matrix products, arithmetic and copies ran while one was open for 12% of the time, Pallas kernels for 0%

commit v1 on v0

v1 whole, which is shorter than its diff:
```python
import functools

import jax
import jax.numpy as jnp
from jax import lax
from jax.experimental import pallas as pl
from jax.experimental.pallas import tpu as pltpu
from jax.sharding import PartitionSpec as P

BLK = 128
F32 = jnp.float32
BF16 = jnp.bfloat16


def mm(left, right):
    return jnp.dot(left, right, preferred_element_type=F32)


def mm_rows(left, right):
    return lax.dot_general(left, right, (((1,), (1,)), ((), ())), preferred_element_type=F32)


def mm_first(left, right):
    return lax.dot_general(left, right, (((0,), (0,)), ((), ())), preferred_element_type=F32)


def largest_tile(size, limit):
    tile = min(limit, size)
    while size % tile:
        tile -= BLK
    return tile


def gather_pair(first, second, product):
    cols = lax.axis_size("cols")
    if cols == 2:
        at_first = lax.axis_index("cols") == 0
        mine = product(
            jnp.where(at_first, first[0], second[0]), jnp.where(at_first, first[1], second[1])
        ).astype(BF16)
        return lax.all_gather(mine, ("cols", "rows"), axis=0, tiled=True)
    return jnp.concatenate(
        [
            lax.all_gather(product(*each).astype(BF16), "rows", axis=0, tiled=True)
            for each in (first, second)
        ]
    )


def place_body(pos1, in1, pos2, in2, u1_ref, u2_ref, link_ref, out_ref):
    at = pl.program_id(0)
    width = u1_ref.shape[1]
    keep1 = in1[at].astype(F32)
    keep2 = in2[at].astype(F32)
    u1 = u1_ref[...]
    linked = mm(u1, link_ref[...])
    out_ref[:width, :] = (-u1.astype(F32) * keep1).T.astype(BF16)
    out_ref[width:, :] = (linked * keep1 - u2_ref[...].astype(F32) * keep2).T.astype(BF16)


def blocks_in_tile(blocks, first_block, block_count):
    ids = first_block + jnp.arange(block_count, dtype=jnp.int32)
    matches = ids[:, None] == blocks[None, :]
    places = jnp.sum(
        jnp.where(matches, jnp.arange(blocks.shape[0], dtype=jnp.int32)[None, :], 0), axis=1
    )
    return places.astype(jnp.int32), jnp.any(matches, axis=1).astype(jnp.int32)


def rows_onto(panel, blocks, first_row, row_count):
    global_rows = first_row + jnp.arange(row_count, dtype=jnp.int32)
    matches = (global_rows // BLK)[:, None] == blocks[None, :]
    places = jnp.sum(
        jnp.where(matches, jnp.arange(blocks.shape[0], dtype=jnp.int32)[None, :], 0), axis=1
    )
    picked = jnp.take(panel, places * BLK + global_rows % BLK, axis=0)
    return jnp.where(jnp.any(matches, axis=1)[:, None], picked, jnp.zeros_like(picked))


def place_panels(both, link, list1, list2, first_row, row_count):
    width = both.shape[1]
    listed = list1.shape[0]
    if row_count % BLK:
        u1 = rows_onto(both[: listed * BLK], list1, first_row, row_count)
        u2 = rows_onto(both[listed * BLK :], list2, first_row, row_count)
        joined = jnp.concatenate([-u1.astype(F32), mm(u1, link) - u2.astype(F32)], axis=1)
        return joined.T.astype(BF16)
    first_block = first_row // BLK
    block_count = row_count // BLK
    pos1, in1 = blocks_in_tile(list1, first_block, block_count)
    pos2, in2 = blocks_in_tile(list2, first_block, block_count)
    return pl.pallas_call(
        place_body,
        out_shape=jax.ShapeDtypeStruct((2 * width, block_count * BLK), BF16),
        grid_spec=pltpu.PrefetchScalarGridSpec(
            num_scalar_prefetch=4,
            grid=(block_count,),
            in_specs=[
                pl.BlockSpec((BLK, width), lambda b, p1, i1, p2, i2: (p1[b], 0)),
                pl.BlockSpec((BLK, width), lambda b, p1, i1, p2, i2: (listed + p2[b], 0)),
                pl.BlockSpec((width, width), lambda b, p1, i1, p2, i2: (0, 0)),
            ],
            out_specs=pl.BlockSpec((2 * width, BLK), lambda b, p1, i1, p2, i2: (0, b)),
        ),
        compiler_params=pltpu.CompilerParams(vmem_limit_bytes=24 * 2**20),
        cost_estimate=pl.CostEstimate(
            flops=2 * block_count * BLK * width * width,
            bytes_accessed=8 * block_count * BLK * width,
            transcendentals=0,
        ),
        name="place_panels",
    )(pos1, in1, pos2, in2, both, both, link)


def lower_body(listed, loc1, in1, loc2, in2, part, *refs):
    tiles1, tiles2 = refs[:listed], refs[listed : 2 * listed]
    l1_ref, v1_ref, l2_ref, out_ref = refs[2 * listed :]
    half = l1_ref.shape[1]
    picked1 = jnp.concatenate(
        [tiles1[k][...] * in1[k].astype(F32).astype(BF16) for k in range(listed)], axis=1
    )
    picked2 = jnp.concatenate(
        [tiles2[k][...] * in2[k].astype(F32).astype(BF16) for k in range(listed)], axis=1
    )
    out_ref[:, :half] = (-mm(picked1, l1_ref[...])).astype(BF16)
    out_ref[:, half:] = (mm(picked1, v1_ref[...]) - mm(picked2, l2_ref[...])).astype(BF16)


def lower_partial(ancestor, both, linked, list1, list2, first_block, part, parts):
    rows, columns = ancestor.shape
    width = both.shape[1]
    half = width // parts
    listed = list1.shape[0]
    depth = listed * BLK
    block_count = columns // BLK
    tile = largest_tile(rows, 512)

    def local(blocks):
        at = blocks - first_block
        inside = jnp.logical_and(at >= 0, at < block_count)
        return jnp.clip(at, 0, block_count - 1), inside.astype(jnp.int32)

    loc1, in1 = local(list1)
    loc2, in2 = local(list2)
    specs = [
        pl.BlockSpec((tile, BLK), functools.partial(lambda k, i, l1, i1, l2, i2, p: (i, l1[k]), k))
        for k in range(listed)
    ] + [
        pl.BlockSpec((tile, BLK), functools.partial(lambda k, i, l1, i1, l2, i2, p: (i, l2[k]), k))
        for k in range(listed)
    ]
    specs += [
        pl.BlockSpec((depth, half), lambda i, l1, i1, l2, i2, p: (0, p[0])),
        pl.BlockSpec((depth, half), lambda i, l1, i1, l2, i2, p: (0, p[0])),
        pl.BlockSpec((depth, half), lambda i, l1, i1, l2, i2, p: (1, p[0])),
    ]
    return pl.pallas_call(
        functools.partial(lower_body, listed),
        out_shape=jax.ShapeDtypeStruct((rows, 2 * half), BF16),
        grid_spec=pltpu.PrefetchScalarGridSpec(
            num_scalar_prefetch=5,
            grid=(rows // tile,),
            in_specs=specs,
            out_specs=pl.BlockSpec((tile, 2 * half), lambda i, l1, i1, l2, i2, p: (i, 0)),
        ),
        compiler_params=pltpu.CompilerParams(vmem_limit_bytes=40 * 2**20),
        cost_estimate=pl.CostEstimate(
            flops=6 * rows * depth * half,
            bytes_accessed=4 * rows * depth + 6 * depth * half,
            transcendentals=0,
        ),
        name="lower_partial",
    )(
        loc1, in1, loc2, in2, jnp.reshape(part, (1,)).astype(jnp.int32),
        *([ancestor] * (2 * listed)), both, linked, both,
    )


def strip_body(strip, w_ref, a_ref, *refs):
    total = mm(w_ref[...], a_ref[...])
    for ref in refs[:-1]:
        total = total + ref[...].astype(F32)
    refs[-1][...] = total.astype(BF16)


def strip_product(ancestor, placed, strip, strips, *added):
    rows, columns = ancestor.shape
    strip_width = columns // strips
    height = placed.shape[0]
    if strip_width % BLK:
        total = mm(
            placed, lax.dynamic_slice_in_dim(ancestor, strip * strip_width, strip_width, 1)
        )
        for each in added:
            total = total + each.astype(F32)
        return total.astype(BF16)
    tile = largest_tile(strip_width, 256)
    per = strip_width // tile
    return pl.pallas_call(
        strip_body,
        out_shape=jax.ShapeDtypeStruct((height, strip_width), BF16),
        grid_spec=pltpu.PrefetchScalarGridSpec(
            num_scalar_prefetch=1,
            grid=(per,),
            in_specs=[
                pl.BlockSpec((height, rows), lambda j, s: (0, 0)),
                pl.BlockSpec((rows, tile), lambda j, s: (0, s[0] * per + j)),
            ]
            + [pl.BlockSpec((height, tile), lambda j, s: (0, j))] * len(added),
            out_specs=pl.BlockSpec((height, tile), lambda j, s: (0, j)),
        ),
        compiler_params=pltpu.CompilerParams(vmem_limit_bytes=40 * 2**20),
        cost_estimate=pl.CostEstimate(
            flops=2 * height * rows * strip_width,
            bytes_accessed=2 * (rows * strip_width + height * rows)
            + 2 * (1 + len(added)) * height * strip_width,
            transcendentals=0,
        ),
        name="strip_product",
    )(jnp.reshape(strip, (1,)).astype(jnp.int32), placed, ancestor, *added)


def add_pair(left, right):
    return (left.astype(F32) + right.astype(F32)).astype(BF16)


def upper_sums(ancestor, placed):
    strips = lax.axis_size("rows")
    row_at = lax.axis_index("rows")
    inner = 4 if strips % 4 == 0 else 1
    if inner == 1:
        whole = strip_product(ancestor, placed, 0, 1)
        return lax.psum_scatter(whole.astype(F32), "rows", scatter_dimension=1, tiled=True)
    depth = strips // inner
    core, side, level = row_at % 2, (row_at // 2) % 2, row_at // 4
    to_core = [(i, i ^ 1) for i in range(strips)]
    to_side = [(i, i ^ 2) for i in range(strips)]
    order = [sorted(range(depth), key=lambda d: (-abs(d - z), d)) for z in range(depth)]
    place = [[order[z].index(d) for d in range(depth)] for z in range(depth)]
    order_table = jnp.array(order, jnp.int32)

    def strip_of(target, x, c):
        return (target * 2 + x) * 2 + c

    layer = []
    for turn in range(depth):
        target = order_table[level, turn]
        far = strip_product(ancestor, placed, strip_of(target, 1 - side, 1 - core), strips)
        far = lax.ppermute(far, "rows", to_core)
        near = strip_product(ancestor, placed, strip_of(target, side, 1 - core), strips)
        near = lax.ppermute(near, "rows", to_core)
        far = strip_product(ancestor, placed, strip_of(target, 1 - side, core), strips, far)
        far = lax.ppermute(far, "rows", to_side)
        layer.append(
            strip_product(ancestor, placed, strip_of(target, side, core), strips, near, far)
        )

    def own_part(step, way):
        gap = depth - 1 - step
        chosen = None
        for z in range(depth):
            target = z + way * gap
            if 0 <= target < depth:
                value = layer[place[z][target]]
                chosen = value if chosen is None else jnp.where(level == z, value, chosen)
        return chosen

    arrived = {1: None, -1: None}
    for step in range(depth - 1):
        gap = depth - 1 - step
        for way in (1, -1):
            senders = [z for z in range(depth) if 0 <= z + way * gap < depth]
            pairs = [
                (z * inner + i, (z + way) * inner + i) for z in senders for i in range(inner)
            ]
            value = own_part(step, way)
            if arrived[way] is not None:
                value = add_pair(value, arrived[way])
            arrived[way] = lax.ppermute(value, "rows", pairs)
    total = layer[-1].astype(F32)
    for way in (1, -1):
        if arrived[way] is not None:
            total = total + arrived[way].astype(F32)
    return total


def body(
    ancestor,
    panel_below,
    panel_beside,
    inverse_lower,
    inverse_upper,
    list_below,
    list_beside,
    second_below,
    second_beside,
    linked_below,
    linked_beside,
    second_lower,
    second_upper,
    blocks_below,
    blocks_beside,
):
    row_at = lax.axis_index("rows")
    col_at = lax.axis_index("cols")
    cols = lax.axis_size("cols")
    tile_rows, tile_cols = ancestor.shape
    width = inverse_lower.shape[0]
    half = width // cols

    beside = gather_pair((panel_beside, inverse_upper), (second_beside, second_upper), mm_rows)
    below = gather_pair((panel_below, inverse_lower), (second_below, second_lower), mm)
    link_below = mm(linked_below, second_lower).astype(BF16)
    link_beside = mm_rows(linked_beside, second_upper).astype(BF16)

    placed = place_panels(
        beside, link_beside, list_beside, blocks_beside,
        row_at * tile_rows, tile_rows,
    )
    upper = upper_sums(ancestor, placed)
    new_upper = upper[:width].T.astype(BF16)
    next_upper = upper[width:].T.astype(BF16)

    depth = below.shape[0] // 2
    linked = mm(below[:depth], link_below).astype(BF16)
    lower_total = None
    sums_total = None
    for shift in reversed(range(cols)):
        part = (col_at + shift) % cols
        piece = lower_partial(
            ancestor, below, linked, list_below, blocks_below,
            col_at * (tile_cols // BLK), part, cols,
        )
        sums = jnp.concatenate(
            [mm(placed[:width], piece), mm(placed[width:], piece[:, half:])], axis=1
        )
        if shift:
            pairs = [(i, (i + shift) % cols) for i in range(cols)]
            piece = lax.ppermute(piece, "cols", pairs)
            sums = lax.ppermute(sums, "cols", pairs)
        piece = piece.astype(F32)
        lower_total = piece if lower_total is None else lower_total + piece
        sums_total = sums if sums_total is None else sums_total + sums
    new_lower = lower_total[:, :half].astype(BF16)
    next_lower = lower_total[:, half:].astype(BF16)

    sums = lax.psum(sums_total, "rows")

    def own(matrix):
        return lax.dynamic_slice_in_dim(matrix, col_at * half, half, 1)

    base = mm(inverse_upper, inverse_lower).astype(BF16)
    base_link = mm(base, own(link_below))
    new_diagonal = (mm(inverse_upper, own(inverse_lower)) + sums[:, :half]).astype(BF16)
    link_part = (sums[:, half : 2 * half] - base_link).astype(BF16)
    next_link = lax.all_gather(link_part, "cols", axis=1, tiled=True)
    next_diagonal = (
        mm(second_upper, own(second_lower))
        + mm_first(link_beside, base_link.astype(BF16))
        + sums[:, 2 * half :]
    ).astype(BF16)
    return (new_lower, new_upper, new_diagonal, next_lower, next_upper, next_link, next_diagonal)


def solution(mesh):
    return jax.shard_map(
        body,
        mesh=mesh,
        in_specs=(
            P("rows", "cols"),
            P("rows", None),
            P("rows", None),
            P(),
            P(),
            P(),
            P(),
            P("rows", None),
            P("rows", None),
            P(),
            P(),
            P(),
            P(),
            P(),
            P(),
        ),
        out_specs=(
            P("rows", "cols"),
            P(("cols", "rows"), None),
            P(None, "cols"),
            P("rows", "cols"),
            P(("cols", "rows"), None),
            P(),
            P(None, "cols"),
        ),
        check_vma=False,
    )
```

time: 1310 us -> 383 us (0.29)
  waiting for transfers between devices: 1010 us -> 162 us
  local copies, waits for them, and re-layouts: 203 us -> 14.8 us
  Pallas kernels: 0 us -> 112 us
  starting transfers between devices: 8.28 us -> 30.4 us
  matrix products: 43.9 us -> 21.8 us
    all_gather x4 -> x2, waiting for transfers between devices: 734 us -> 82.5 us  [gather_pair(): return lax.all_gather(mine, ('cols', 'rows'), axis=0, tiled=True)]
    psum x2 -> x1, waiting for transfers between devices: 207 us -> 49.7 us  [body(): sums = lax.psum(sums_total, 'rows')]
    pallas_call x0 -> x19, Pallas kernels: none -> 112 us  [the longest x16 83 us: strip_product(): pl.pallas_call(strip_body, out_shape=jax.ShapeDtypeStruct((height, strip_...]
    reduce_scatter x2 -> x0, waiting for transfers between devices: 71.5 us -> none  [lower_block(): lax.psum_scatter(partial_value, 'cols', scatter_dimension=1, tiled=True)]
    all_to_all x1 -> x0, local copies, waits for them, and re-layouts: 48.7 us -> none  [body(): lax.all_to_all(ancestor, 'rows', split_axis=1, concat_axis=0, tiled=True)]
    reshape x1 -> x0, local copies, waits for them, and re-layouts: 43.8 us -> none  [listed_columns(): tile.reshape(tile.shape[0], block_count, BLK)]
    unnamed x49 -> x55, local copies, waits for them, and re-layouts: 53.1 us -> 10.8 us
    gather x7 -> x0, local copies, waits for them, and re-layouts: 39.7 us -> none  [the longest x3 17.4 us: rows_onto(): picked = jnp.take(panel, position * BLK + offset, axis=0)]
  transfers between devices with their start and end apart: 9 -> 23, of which waited for: 8 -> 7; matrix products, arithmetic and copies ran while one was open for 12% -> 10% of each run, Pallas kernels for 0% -> 29%
where the time goes in v1:
time: 383 us; the launch traced here: 381 us
  waiting for transfers between devices  162 us (42%)
  Pallas kernels  112 us (29%)
  starting transfers between devices  30.4 us (8%)
  matrix products  21.8 us (6%)
  between operations  17.1 us (4%)
  local copies, waits for them, and re-layouts  14.8 us (4%)
  other arithmetic  14.7 us (4%)
  blocking collectives  8.17 us (2%)
    pallas_call x16, Pallas kernels, strip_product(): pl.pallas_call(strip_body, out_shape=jax.ShapeDtypeStruct((height, strip_...  83 us
    all_gather x2, waiting for transfers between devices, gather_pair(): return lax.all_gather(mine, ('cols', 'rows'), axis=0, tiled=True)  82.5 us
    psum x1, waiting for transfers between devices, body(): sums = lax.psum(sums_total, 'rows')  49.7 us
    pallas_call x2, Pallas kernels, lower_partial(): pl.pallas_call(functools.partial(lower_body, listed), out_shape=jax.Shape...  24.3 us
    ppermute x6, starting transfers between devices, upper_sums(): arrived[way] = lax.ppermute(value, 'rows', pairs)  20 us
    dot_general x10, matrix products, mm(): return jnp.dot(left, right, preferred_element_type=F32)  15.9 us
    ppermute x1, waiting for transfers between devices, body(): piece = lax.ppermute(piece, 'cols', pairs)  15.1 us
    unnamed x55, local copies, waits for them, and re-layouts  10.8 us
  transfers between devices with their start and end apart: 23, of which 7 were waited for; matrix products, arithmetic and copies ran while one was open for 10% of the time, Pallas kernels for 29%

profile of v1, /device:TPU:0, one launch (start us, length us, event | category | flops | bytes accessed | tf_op | source)
XLA Modules:
  0.0 381.2 jit_solution(7002729444678278709)
XLA Ops:
  15.8 60.5 %all-gather.5.cloned.1.call-done.u1_ref.u2_ref = bf16[4096,512]{1,0:T(8,128)(2,1)} async-done(((bf16[128,512]{1,0:T(8,128)(2,1)}), bf16[4096,512]{1,0:T(8,128)(2,1)}) %all-gather.5.cloned.1.call-update) | async-done | bytes 4194320 | tf_op jit(solution)/shard_map/all_gather | solution.py:41
  79.5 4.8 %place_panels.1.w_ref = bf16[1024,1536]{1,0:T(8,128)(2,1)S(1)} custom-call(s32[12]{0:T(128)S(1)} %get-tuple-element.24.pos1, s32[12]{0:T(128)S(1)} %convert_element_type.112.in1, s32[12]{0:T(128)S(1)} %get-tuple-element.23.pos2, s32[12]{0:T(128)S(1)} %convert_element_type.113.in2, bf16[4096,512]{1,0:T(8,128)(2,1)S(1)} %copy-done.3, ...), custom_call_target="tpu_custom_call" | custom-call | flops 805306368 | bytes 6291456 | tf_op jit(solution)/shard_map/place_panels/pallas_call | solution.py:92
  84.3 5.3 %strip_product.25 = bf16[1024,768]{1,0:T(8,128)(2,1)} custom-call(s32[1]{0:T(128)} %bitcast.16.strip, bf16[1024,1536]{1,0:T(8,128)(2,1)S(1)} %place_panels.1.w_ref, bf16[1536,12288]{1,0:T(8,128)(2,1)} %a_ref.31), custom_call_target="tpu_custom_call" | custom-call | flops 2415919104 | bytes 7077888 | tf_op jit(solution)/shard_map/strip_product/pallas_call | solution.py:199
  96.2 5.3 %strip_product.29 = bf16[1024,768]{1,0:T(8,128)(2,1)} custom-call(s32[1]{0:T(128)} %bitcast.21.strip, bf16[1024,1536]{1,0:T(8,128)(2,1)S(1)} %place_panels.1.w_ref, bf16[1536,12288]{1,0:T(8,128)(2,1)} %a_ref.31), custom_call_target="tpu_custom_call" | custom-call | flops 2415919104 | bytes 7077888 | tf_op jit(solution)/shard_map/strip_product/pallas_call | solution.py:199
  101.8 5.2 %strip_product.28 = bf16[1024,768]{1,0:T(8,128)(2,1)} custom-call(s32[1]{0:T(128)} %bitcast.19.strip, bf16[1024,1536]{1,0:T(8,128)(2,1)S(1)} %place_panels.1.w_ref, bf16[1536,12288]{1,0:T(8,128)(2,1)} %a_ref.31), custom_call_target="tpu_custom_call" | custom-call | flops 2415919104 | bytes 7077888 | tf_op jit(solution)/shard_map/strip_product/pallas_call | solution.py:199
  107.3 5.3 %strip_product.24 = bf16[1024,768]{1,0:T(8,128)(2,1)} custom-call(s32[1]{0:T(128)} %bitcast.14.strip, bf16[1024,1536]{1,0:T(8,128)(2,1)S(1)} %place_panels.1.w_ref, bf16[1536,12288]{1,0:T(8,128)(2,1)} %a_ref.31), custom_call_target="tpu_custom_call" | custom-call | flops 2415919104 | bytes 7077888 | tf_op jit(solution)/shard_map/strip_product/pallas_call | solution.py:199
  112.8 5.3 %strip_product.21 = bf16[1024,768]{1,0:T(8,128)(2,1)} custom-call(s32[1]{0:T(128)} %bitcast.11.strip, bf16[1024,1536]{1,0:T(8,128)(2,1)S(1)} %place_panels.1.w_ref, bf16[1536,12288]{1,0:T(8,128)(2,1)} %a_ref.31), custom_call_target="tpu_custom_call" | custom-call | flops 2415919104 | bytes 7077888 | tf_op jit(solution)/shard_map/strip_product/pallas_call | solution.py:199
  118.3 22.0 %all-gather.3.cloned.1.call-done.refs_32_.refs_34_ = bf16[4096,512]{1,0:T(8,128)(2,1)} async-done(((bf16[128,512]{1,0:T(8,128)(2,1)}), bf16[4096,512]{1,0:T(8,128)(2,1)}) %all-gather.3.cloned.1.call-update) | async-done | bytes 4194320 | tf_op jit(solution)/shard_map/all_gather | solution.py:41
  143.3 5.7 %strip_product.26 = bf16[1024,768]{1,0:T(8,128)(2,1)} custom-call(s32[1]{0:T(128)} %bitcast.15.strip, bf16[1024,1536]{1,0:T(8,128)(2,1)S(1)} %place_panels.1.w_ref, bf16[1536,12288]{1,0:T(8,128)(2,1)} %a_ref.31, bf16[1024,768]{1,0:T(8,128)(2,1)} %collective-permute-done.8.refs_0_), custom_call_target="tpu_custom_call" | custom-call | flops 2415919104 | bytes 8650752 | tf_op jit(solution)/shard_map/strip_product/pallas_call | solution.py:199
  150.3 12.4 %lower_partial.2 = bf16[1536,512]{1,0:T(8,128)(2,1)} custom-call(s32[16]{0:T(128)S(1)} %get-tuple-element.40.loc1, s32[16]{0:T(128)S(1)} %get-tuple-element.38.in1, s32[16]{0:T(128)S(1)} %get-tuple-element.39.loc2, s32[16]{0:T(128)S(1)} %get-tuple-element.37.in2, s32[1]{0:T(128)} %bitcast.part, bf16[1536,12288]{1,0:T(8,128)(2,1)} %a_ref.31, ...), custom_call_target="tpu_custom_call" | custom-call | flops 4831838208 | bytes 15728640 | tf_op jit(solution)/shard_map/lower_partial/pallas_call | solution.py:157
  166.1 11.9 %lower_partial.3 = bf16[1536,512]{1,0:T(8,128)(2,1)S(1)} custom-call(s32[16]{0:T(128)S(1)} %get-tuple-element.40.loc1, s32[16]{0:T(128)S(1)} %get-tuple-element.38.in1, s32[16]{0:T(128)S(1)} %get-tuple-element.39.loc2, s32[16]{0:T(128)S(1)} %get-tuple-element.37.in2, s32[1]{0:T(128)} %bitcast.1.part, bf16[1536,12288]{1,0:T(8,128)(2,1)} %a_ref.31, ...), custom_call_target="tpu_custom_call" | custom-call | flops 4831838208 | bytes 15728640 | tf_op jit(solution)/shard_map/lower_partial/pallas_call | solution.py:157
  178.0 5.2 %strip_product.30 = bf16[1024,768]{1,0:T(8,128)(2,1)S(1)} custom-call(s32[1]{0:T(128)} %bitcast.20.strip, bf16[1024,1536]{1,0:T(8,128)(2,1)S(1)} %place_panels.1.w_ref, bf16[1536,12288]{1,0:T(8,128)(2,1)} %a_ref.31, bf16[1024,768]{1,0:T(8,128)(2,1)} %collective-permute-done.11.refs_0_), custom_call_target="tpu_custom_call" | custom-call | flops 2415919104 | bytes 8650752 | tf_op jit(solution)/shard_map/strip_product/pallas_call | solution.py:199
  185.9 5.0 %strip_product.27 = bf16[1024,768]{1,0:T(8,128)(2,1)S(1)} custom-call(s32[1]{0:T(128)} %bitcast.13.strip, bf16[1024,1536]{1,0:T(8,128)(2,1)S(1)} %place_panels.1.w_ref, bf16[1536,12288]{1,0:T(8,128)(2,1)} %a_ref.31, bf16[1024,768]{1,0:T(8,128)(2,1)} %collective-permute-done.7.refs_0_, bf16[1024,768]{1,0:T(8,128)(2,1)} %collective-permute-done.9.refs_1_), custom_call_target="tpu_custom_call" | custom-call | flops 2415919104 | bytes 10223616 | tf_op jit(solution)/shard_map/strip_product/pallas_call | solution.py:199
  202.1 5.3 %strip_product.20 = bf16[1024,768]{1,0:T(8,128)(2,1)} custom-call(s32[1]{0:T(128)} %bitcast.9.strip, bf16[1024,1536]{1,0:T(8,128)(2,1)S(1)} %place_panels.1.w_ref, bf16[1536,12288]{1,0:T(8,128)(2,1)} %a_ref.31), custom_call_target="tpu_custom_call" | custom-call | flops 2415919104 | bytes 7077888 | tf_op jit(solution)/shard_map/strip_product/pallas_call | solution.py:199
  209.1 10.5 %collective-permute-done.12.refs_1_ = bf16[1024,768]{1,0:T(8,128)(2,1)S(1)} collective-permute-done((bf16[1024,768]{1,0:T(8,128)(2,1)S(1)}, bf16[1024,768]{1,0:T(8,128)(2,1)S(1)}, u32[]{:S(2)}, u32[]{:S(2)}) %collective-permute-start.12) | collective-permute-done | bytes 1572896 | tf_op jit(solution)/shard_map/ppermute | solution.py:253
  221.2 5.6 %strip_product.22 = bf16[1024,768]{1,0:T(8,128)(2,1)} custom-call(s32[1]{0:T(128)} %bitcast.10.strip, bf16[1024,1536]{1,0:T(8,128)(2,1)S(1)} %place_panels.1.w_ref, bf16[1536,12288]{1,0:T(8,128)(2,1)} %a_ref.31, bf16[1024,768]{1,0:T(8,128)(2,1)} %collective-permute-done.5.refs_0_), custom_call_target="tpu_custom_call" | custom-call | flops 2415919104 | bytes 8650752 | tf_op jit(solution)/shard_map/strip_product/pallas_call | solution.py:199
  242.1 5.3 %strip_product.16 = bf16[1024,768]{1,0:T(8,128)(2,1)} custom-call(s32[1]{0:T(128)} %bitcast.4.strip, bf16[1024,1536]{1,0:T(8,128)(2,1)S(1)} %place_panels.1.w_ref, bf16[1536,12288]{1,0:T(8,128)(2,1)} %a_ref.31), custom_call_target="tpu_custom_call" | custom-call | flops 2415919104 | bytes 7077888 | tf_op jit(solution)/shard_map/strip_product/pallas_call | solution.py:199
  250.4 5.5 %strip_product.18 = bf16[1024,768]{1,0:T(8,128)(2,1)} custom-call(s32[1]{0:T(128)} %bitcast.5.strip, bf16[1024,1536]{1,0:T(8,128)(2,1)S(1)} %place_panels.1.w_ref, bf16[1536,12288]{1,0:T(8,128)(2,1)} %a_ref.31, bf16[1024,768]{1,0:T(8,128)(2,1)S(1)} %copy-done.10), custom_call_target="tpu_custom_call" | custom-call | flops 2415919104 | bytes 8650752 | tf_op jit(solution)/shard_map/strip_product/pallas_call | solution.py:199
  255.8 15.1 %collective-permute-done = bf16[1536,512]{1,0:T(8,128)(2,1)} collective-permute-done((bf16[1536,512]{1,0:T(8,128)(2,1)}, bf16[1536,512]{1,0:T(8,128)(2,1)}, u32[]{:S(2)}, u32[]{:S(2)}) %collective-permute-start) | collective-permute-done | bytes 1572896 | tf_op jit(solution)/shard_map/ppermute | solution.py:339
  273.9 5.1 %strip_product.23 = bf16[1024,768]{1,0:T(8,128)(2,1)S(1)} custom-call(s32[1]{0:T(128)} %bitcast.8.strip, bf16[1024,1536]{1,0:T(8,128)(2,1)S(1)} %place_panels.1.w_ref, bf16[1536,12288]{1,0:T(8,128)(2,1)} %a_ref.31, bf16[1024,768]{1,0:T(8,128)(2,1)} %collective-permute-done.4.refs_0_, bf16[1024,768]{1,0:T(8,128)(2,1)} %collective-permute-done.6.refs_1_), custom_call_target="tpu_custom_call" | custom-call | flops 2415919104 | bytes 10223616 | tf_op jit(solution)/shard_map/strip_product/pallas_call | solution.py:199
  287.7 8.2 %collective-permute-start.15 = (bf16[1024,768]{1,0:T(8,128)(2,1)}, bf16[1024,768]{1,0:T(8,128)(2,1)}, u32[]{:S(2)}, u32[]{:S(2)}) collective-permute-start(bf16[1024,768]{1,0:T(8,128)(2,1)} %get-tuple-element.31), channel_id=1, source_target_pairs={{0,8},{2,10},{4,12},{6,14},{8,16},{10,18},{12,20},{14,22},{16,24},... | collective-permute-start | bytes 4718600 | tf_op jit(solution)/shard_map/ppermute | solution.py:279
  298.5 49.7 %all-reduce.2.cloned.1.call-done = f32[512,768]{0,1:T(8,128)} async-done(((f32[512,768]{0,1:T(8,128)}), f32[512,768]{0,1:T(8,128)}) %all-reduce.2.cloned.1.call-update) | async-done | bytes 1572880 | tf_op jit(solution)/shard_map/psum | solution.py:347
  349.5 8.2 %all_gather.11 = bf16[512,512]{0,1:T(8,128)(2,1)} all-gather(bf16[512,256]{0,1:T(8,128)(2,1)S(1)} %fusion.14), channel_id=1, replica_groups=mesh['rows'=16,'cols'=2] {'cols'}, dimensions={1}, use_global_device_ids=true | all-gather | bytes 786432 | tf_op jit(solution)/shard_map/all_gather | solution.py:356
  364.8 5.0 %strip_product.19 = bf16[1024,768]{1,0:T(8,128)(2,1)S(1)} custom-call(s32[1]{0:T(128)} %bitcast.3.strip, bf16[1024,1536]{1,0:T(8,128)(2,1)S(1)} %place_panels.1.w_ref, bf16[1536,12288]{1,0:T(8,128)(2,1)} %a_ref.31, bf16[1024,768]{1,0:T(8,128)(2,1)} %collective-permute-done.1.refs_0_, bf16[1024,768]{1,0:T(8,128)(2,1)} %collective-permute-done.3.refs_1_), custom_call_target="tpu_custom_call" | custom-call | flops 2415919104 | bytes 10223616 | tf_op jit(solution)/shard_map/strip_product/pallas_call | solution.py:199
  (131 shorter events, 86.9 us)
Async XLA Ops:
  7.2 69.0 %all-gather.5.cloned.1.call-start = ((), (), s32[]{:S(2)}) async-start(), calls=%async_computation.1 | async-start | bytes 4325376 | tf_op jit(solution)/shard_map/all_gather | solution.py:41
  9.6 130.8 %all-gather.3.cloned.1.call-start = ((), (), s32[]{:S(2)}) async-start(), calls=%async_computation | async-start | bytes 4325376 | tf_op jit(solution)/shard_map/all_gather | solution.py:41
  10.6 337.6 %all-reduce.2.cloned.1.call-start = ((), (), s32[]{:S(2)}) async-start(), calls=%async_computation.2 | async-start | bytes 3145728 | tf_op jit(solution)/shard_map/psum | solution.py:347
  14.3 62.0 %copy-start.15 = (bf16[512,512]{1,0:T(8,128)(2,1)}, bf16[512,512]{1,0:T(8,128)(2,1)S(1)}, u32[]{:S(2)}) copy-start(bf16[512,512]{1,0:T(8,128)(2,1)S(1)} %convolution_convert_fusion.3) | copy-start | bytes 1572868
  89.6 53.7 %collective-permute-start.8 = (bf16[1024,768]{1,0:T(8,128)(2,1)}, bf16[1024,768]{1,0:T(8,128)(2,1)}, u32[]{:S(2)}, u32[]{:S(2)}) collective-permute-start(bf16[1024,768]{1,0:T(8,128)(2,1)} %strip_product.25), channel_id=1, source_target_pairs={{0,2},{2,0},{4,6},{6,4},{8,10},{10,8},{12,14},{14,12},{16,18},{18,... | collective-permute-start | bytes 4718600 | tf_op jit(solution)/shard_map/ppermute | solution.py:249
  101.5 76.5 %collective-permute-start.11 = (bf16[1024,768]{1,0:T(8,128)(2,1)}, bf16[1024,768]{1,0:T(8,128)(2,1)}, u32[]{:S(2)}, u32[]{:S(2)}) collective-permute-start(bf16[1024,768]{1,0:T(8,128)(2,1)} %strip_product.29), channel_id=1, source_target_pairs={{0,2},{2,0},{4,6},{6,4},{8,10},{10,8},{12,14},{14,12},{16,18},{18,... | collective-permute-start | bytes 4718600 | tf_op jit(solution)/shard_map/ppermute | solution.py:249
  107.0 92.6 %collective-permute-start.10 = (bf16[1024,768]{1,0:T(8,128)(2,1)}, bf16[1024,768]{1,0:T(8,128)(2,1)}, u32[]{:S(2)}, u32[]{:S(2)}) collective-permute-start(bf16[1024,768]{1,0:T(8,128)(2,1)} %strip_product.28), channel_id=1, source_target_pairs={{0,2},{2,0},{4,6},{6,4},{8,10},{10,8},{12,14},{14,12},{16,18},{18,... | collective-permute-start | bytes 4718600 | tf_op jit(solution)/shard_map/ppermute | solution.py:251
  112.5 73.2 %collective-permute-start.7 = (bf16[1024,768]{1,0:T(8,128)(2,1)}, bf16[1024,768]{1,0:T(8,128)(2,1)}, u32[]{:S(2)}, u32[]{:S(2)}) collective-permute-start(bf16[1024,768]{1,0:T(8,128)(2,1)} %strip_product.24), channel_id=1, source_target_pairs={{0,2},{2,0},{4,6},{6,4},{8,10},{10,8},{12,14},{14,12},{16,18},{18,... | collective-permute-start | bytes 4718600 | tf_op jit(solution)/shard_map/ppermute | solution.py:251
  118.1 81.6 %collective-permute-start.5 = (bf16[1024,768]{1,0:T(8,128)(2,1)}, bf16[1024,768]{1,0:T(8,128)(2,1)}, u32[]{:S(2)}, u32[]{:S(2)}) collective-permute-start(bf16[1024,768]{1,0:T(8,128)(2,1)} %strip_product.21), channel_id=1, source_target_pairs={{0,2},{2,0},{4,6},{6,4},{8,10},{10,8},{12,14},{14,12},{16,18},{18,... | collective-permute-start | bytes 4718600 | tf_op jit(solution)/shard_map/ppermute | solution.py:249
  149.0 36.9 %collective-permute-start.9 = (bf16[1024,768]{1,0:T(8,128)(2,1)}, bf16[1024,768]{1,0:T(8,128)(2,1)}, u32[]{:S(2)}, u32[]{:S(2)}) collective-permute-start(bf16[1024,768]{1,0:T(8,128)(2,1)} %strip_product.26), channel_id=1, source_target_pairs={{0,4},{2,6},{4,0},{6,2},{8,12},{10,14},{12,8},{14,10},{16,20},{18,... | collective-permute-start | bytes 4718600 | tf_op jit(solution)/shard_map/ppermute | solution.py:253
  183.2 36.4 %collective-permute-start.12 = (bf16[1024,768]{1,0:T(8,128)(2,1)S(1)}, bf16[1024,768]{1,0:T(8,128)(2,1)S(1)}, u32[]{:S(2)}, u32[]{:S(2)}) collective-permute-start(bf16[1024,768]{1,0:T(8,128)(2,1)S(1)} %strip_product.30), channel_id=1, source_target_pairs={{0,4},{2,6},{4,0},{6,2},{8,12},{10,14},{12,8},{14,10},{16,20},{18,... | collective-permute-start | bytes 4718600 | tf_op jit(solution)/shard_map/ppermute | solution.py:253
  191.0 40.6 %collective-permute-start.13 = (bf16[1024,768]{1,0:T(8,128)(2,1)S(1)}, bf16[1024,768]{1,0:T(8,128)(2,1)S(1)}, u32[]{:S(2)}, u32[]{:S(2)}) collective-permute-start(bf16[1024,768]{1,0:T(8,128)(2,1)S(1)} %strip_product.27), channel_id=1, source_target_pairs={{0,8},{2,10},{4,12},{6,14},{1,9},{3,11},{5,13},{7,15}} | collective-permute-start | bytes 4718600 | tf_op jit(solution)/shard_map/ppermute | solution.py:279
  194.4 37.2 %collective-permute-start.16 = (bf16[1024,768]{1,0:T(8,128)(2,1)S(1)}, bf16[1024,768]{1,0:T(8,128)(2,1)S(1)}, u32[]{:S(2)}, u32[]{:S(2)}) collective-permute-start(bf16[1024,768]{1,0:T(8,128)(2,1)S(1)} %strip_product.27), channel_id=1, source_target_pairs={{24,16},{26,18},{28,20},{30,22},{25,17},{27,19},{29,21},{31,23}} | collective-permute-start | bytes 4718600 | tf_op jit(solution)/shard_map/ppermute | solution.py:279
  199.6 36.2 %collective-permute-start.2 = (bf16[1024,768]{1,0:T(8,128)(2,1)S(1)}, bf16[1024,768]{1,0:T(8,128)(2,1)S(1)}, u32[]{:S(2)}, u32[]{:S(2)}) collective-permute-start(bf16[1024,768]{1,0:T(8,128)(2,1)S(1)} %strip_product.17), channel_id=1, source_target_pairs={{0,2},{2,0},{4,6},{6,4},{8,10},{10,8},{12,14},{14,12},{16,18},{18,... | collective-permute-start | bytes 4718600 | tf_op jit(solution)/shard_map/ppermute | solution.py:249
  199.7 40.5 %collective-permute-start.19 = (f32[512,768]{0,1:T(8,128)S(1)}, f32[512,768]{0,1:T(8,128)S(1)}, u32[]{:S(2)}, u32[]{:S(2)}) collective-permute-start(f32[512,768]{0,1:T(8,128)S(1)} %pad_maximum_fusion), channel_id=1, source_target_pairs={{0,1},{1,0},{2,3},{3,2},{4,5},{5,4},{6,7},{7,6},{8,9},{9,8},{10,11... | collective-permute-start | bytes 4718600 | tf_op jit(solution)/shard_map/ppermute | solution.py:340
  219.5 51.4 %collective-permute-start = (bf16[1536,512]{1,0:T(8,128)(2,1)}, bf16[1536,512]{1,0:T(8,128)(2,1)}, u32[]{:S(2)}, u32[]{:S(2)}) collective-permute-start(bf16[1536,512]{1,0:T(8,128)(2,1)} %lower_partial.2), channel_id=1, source_target_pairs={{0,1},{1,0},{2,3},{3,2},{4,5},{5,4},{6,7},{7,6},{8,9},{9,8},{10,11... | collective-permute-start | bytes 4718600 | tf_op jit(solution)/shard_map/ppermute | solution.py:339
  231.5 41.2 %collective-permute-start.4 = (bf16[1024,768]{1,0:T(8,128)(2,1)}, bf16[1024,768]{1,0:T(8,128)(2,1)}, u32[]{:S(2)}, u32[]{:S(2)}) collective-permute-start(bf16[1024,768]{1,0:T(8,128)(2,1)} %strip_product.20), channel_id=1, source_target_pairs={{0,2},{2,0},{4,6},{6,4},{8,10},{10,8},{12,14},{14,12},{16,18},{18,... | collective-permute-start | bytes 4718600 | tf_op jit(solution)/shard_map/ppermute | solution.py:251
  231.6 42.3 %collective-permute-start.6 = (bf16[1024,768]{1,0:T(8,128)(2,1)}, bf16[1024,768]{1,0:T(8,128)(2,1)}, u32[]{:S(2)}, u32[]{:S(2)}) collective-permute-start(bf16[1024,768]{1,0:T(8,128)(2,1)} %strip_product.22), channel_id=1, source_target_pairs={{0,4},{2,6},{4,0},{6,2},{8,12},{10,14},{12,8},{14,10},{16,20},{18,... | collective-permute-start | bytes 4718600 | tf_op jit(solution)/shard_map/ppermute | solution.py:253
  235.8 47.4 %collective-permute-start.14 = (bf16[1024,768]{1,0:T(8,128)(2,1)}, bf16[1024,768]{1,0:T(8,128)(2,1)}, u32[]{:S(2)}, u32[]{:S(2)}) collective-permute-start(bf16[1024,768]{1,0:T(8,128)(2,1)} %get-tuple-element.25), channel_id=1, source_target_pairs={{0,8},{2,10},{4,12},{6,14},{8,16},{10,18},{12,20},{14,22},{1,9},{3... | collective-permute-start | bytes 4718600 | tf_op jit(solution)/shard_map/ppermute | solution.py:279
  240.3 43.0 %collective-permute-start.17 = (bf16[1024,768]{1,0:T(8,128)(2,1)}, bf16[1024,768]{1,0:T(8,128)(2,1)}, u32[]{:S(2)}, u32[]{:S(2)}) collective-permute-start(bf16[1024,768]{1,0:T(8,128)(2,1)} %get-tuple-element.26), channel_id=1, source_target_pairs={{16,8},{18,10},{20,12},{22,14},{24,16},{26,18},{28,20},{30,22},{17... | collective-permute-start | bytes 4718600 | tf_op jit(solution)/shard_map/ppermute | solution.py:279
  270.9 93.9 %collective-permute-start.1 = (bf16[1024,768]{1,0:T(8,128)(2,1)}, bf16[1024,768]{1,0:T(8,128)(2,1)}, u32[]{:S(2)}, u32[]{:S(2)}) collective-permute-start(bf16[1024,768]{1,0:T(8,128)(2,1)} %strip_product.16), channel_id=1, source_target_pairs={{0,2},{2,0},{4,6},{6,4},{8,10},{10,8},{12,14},{14,12},{16,18},{18,... | collective-permute-start | bytes 4718600 | tf_op jit(solution)/shard_map/ppermute | solution.py:251
  272.8 92.1 %collective-permute-start.3 = (bf16[1024,768]{1,0:T(8,128)(2,1)}, bf16[1024,768]{1,0:T(8,128)(2,1)}, u32[]{:S(2)}, u32[]{:S(2)}) collective-permute-start(bf16[1024,768]{1,0:T(8,128)(2,1)} %strip_product.18), channel_id=1, source_target_pairs={{0,4},{2,6},{4,0},{6,2},{8,12},{10,14},{12,8},{14,10},{16,20},{18,... | collective-permute-start | bytes 4718600 | tf_op jit(solution)/shard_map/ppermute | solution.py:253
  287.7 82.1 %collective-permute-start.15 = (bf16[1024,768]{1,0:T(8,128)(2,1)}, bf16[1024,768]{1,0:T(8,128)(2,1)}, u32[]{:S(2)}, u32[]{:S(2)}) collective-permute-start(bf16[1024,768]{1,0:T(8,128)(2,1)} %get-tuple-element.31), channel_id=1, source_target_pairs={{0,8},{2,10},{4,12},{6,14},{8,16},{10,18},{12,20},{14,22},{16,24},... | collective-permute-start | bytes 4718600 | tf_op jit(solution)/shard_map/ppermute | solution.py:279
  295.9 73.9 %collective-permute-start.18 = (bf16[1024,768]{1,0:T(8,128)(2,1)}, bf16[1024,768]{1,0:T(8,128)(2,1)}, u32[]{:S(2)}, u32[]{:S(2)}) collective-permute-start(bf16[1024,768]{1,0:T(8,128)(2,1)} %get-tuple-element.32), channel_id=1, source_target_pairs={{8,0},{10,2},{12,4},{14,6},{16,8},{18,10},{20,12},{22,14},{24,16},... | collective-permute-start | bytes 4718600 | tf_op jit(solution)/shard_map/ppermute | solution.py:279
  (24 other events, 146.1 us)
Sparse Core Ops, SparseCore 0:
  11.5 64.7 all-gather.4
  79.7 60.6 all-gather.2
  249.1 99.1 all-reduce.1

commit v2 on v1

--- a/solution.py
+++ b/solution.py
@@ -112,68 +112,85 @@
     )(pos1, in1, pos2, in2, both, both, link)
 
 
-def lower_body(listed, loc1, in1, loc2, in2, part, *refs):
-    tiles1, tiles2 = refs[:listed], refs[listed : 2 * listed]
-    l1_ref, v1_ref, l2_ref, out_ref = refs[2 * listed :]
-    half = l1_ref.shape[1]
-    picked1 = jnp.concatenate(
-        [tiles1[k][...] * in1[k].astype(F32).astype(BF16) for k in range(listed)], axis=1
-    )
-    picked2 = jnp.concatenate(
-        [tiles2[k][...] * in2[k].astype(F32).astype(BF16) for k in range(listed)], axis=1
-    )
-    out_ref[:, :half] = (-mm(picked1, l1_ref[...])).astype(BF16)
-    out_ref[:, half:] = (mm(picked1, v1_ref[...]) - mm(picked2, l2_ref[...])).astype(BF16)
-
-
-def lower_partial(ancestor, both, linked, list1, list2, first_block, part, parts):
+SLOTS = 4
+FREE = pl.CostEstimate(flops=0, bytes_accessed=0, transcendentals=0)
+ANY = pl.BlockSpec(memory_space=pl.ANY)
+
+
+def lower_slots_body(groups, block_count, l1, l2, at, *refs):
+    listed = groups * SLOTS
+    tiles = (refs[:listed], refs[listed : 2 * listed])
+    panel_refs, link_ref = refs[2 * listed : 2 * listed + 2], refs[2 * listed + 2]
+    given_ref, kept_ref, linked_ref, total_ref = refs[-4:]
+    width = link_ref.shape[0]
+    half = width // 2
+
+    @pl.when(pl.program_id(0) == 0)
+    def _():
+        linked_ref[...] = mm(panel_refs[0][...], link_ref[...]).astype(BF16)
+
+    def picked(which, blocks):
+        kept = []
+        for k in range(listed):
+            place = blocks[k] - at[0]
+            inside = jnp.logical_and(place >= 0, place < block_count)
+            kept.append(tiles[which][k][...] * jnp.where(inside, 1.0, 0.0).astype(BF16))
+        return jnp.concatenate(kept, axis=1)
+
+    picked1 = picked(0, l1)
+    total_ref[:, :width] = -mm(picked1, panel_refs[0][...])
+    second = mm(picked1, linked_ref[...]) - mm(picked(1, l2), panel_refs[1][...])
+    total_ref[:, width:] = second
+
+    for column, (own, other) in ((0, (kept_ref, given_ref)), (1, (given_ref, kept_ref))):
+
+        @pl.when(at[1] == column)
+        def _():
+            for out, start in ((own, 0), (other, half)):
+                out[:, :half] = total_ref[:, start : start + half].astype(BF16)
+                second = total_ref[:, width + start : width + start + half]
+                out[:, half:] = second.astype(BF16)
+
+
+def lower_slots(ancestor, panels, link, list1, list2, first_block, column, first):
     rows, columns = ancestor.shape
-    width = both.shape[1]
-    half = width // parts
-    listed = list1.shape[0]
-    depth = listed * BLK
+    listed, width = list1.shape[0], link.shape[0]
     block_count = columns // BLK
     tile = largest_tile(rows, 512)
-
-    def local(blocks):
-        at = blocks - first_block
-        inside = jnp.logical_and(at >= 0, at < block_count)
-        return jnp.clip(at, 0, block_count - 1), inside.astype(jnp.int32)
-
-    loc1, in1 = local(list1)
-    loc2, in2 = local(list2)
-    specs = [
-        pl.BlockSpec((tile, BLK), functools.partial(lambda k, i, l1, i1, l2, i2, p: (i, l1[k]), k))
-        for k in range(listed)
-    ] + [
-        pl.BlockSpec((tile, BLK), functools.partial(lambda k, i, l1, i1, l2, i2, p: (i, l2[k]), k))
-        for k in range(listed)
+    at = jnp.stack([first_block, column]).astype(jnp.int32)
+
+    def picked(which, k):
+        def index(i, l1, l2, at):
+            place = (l1, l2)[which][k] - at[0]
+            inside = jnp.logical_and(place >= 0, place < block_count)
+            return jnp.where(inside, i, 0), jnp.clip(place, 0, block_count - 1)
+
+        return pl.BlockSpec((tile, BLK), index)
+
+    specs = [picked(which, k) for which in (0, 1) for k in range(listed)]
+    specs += [
+        pl.BlockSpec((listed * BLK, width), lambda i, l1, l2, at: (0, 0)),
+        pl.BlockSpec((listed * BLK, width), lambda i, l1, l2, at: (1, 0)),
+        pl.BlockSpec((width, width), lambda i, l1, l2, at: (0, 0)),
     ]
-    specs += [
-        pl.BlockSpec((depth, half), lambda i, l1, i1, l2, i2, p: (0, p[0])),
-        pl.BlockSpec((depth, half), lambda i, l1, i1, l2, i2, p: (0, p[0])),
-        pl.BlockSpec((depth, half), lambda i, l1, i1, l2, i2, p: (1, p[0])),
-    ]
+    shape = jax.ShapeDtypeStruct((rows, width), BF16)
     return pl.pallas_call(
-        functools.partial(lower_body, listed),
-        out_shape=jax.ShapeDtypeStruct((rows, 2 * half), BF16),
+        functools.partial(lower_slots_body, listed // SLOTS, block_count),
+        out_shape=(shape, shape),
         grid_spec=pltpu.PrefetchScalarGridSpec(
-            num_scalar_prefetch=5,
+            num_scalar_prefetch=3,
             grid=(rows // tile,),
-            in_specs=specs,
-            out_specs=pl.BlockSpec((tile, 2 * half), lambda i, l1, i1, l2, i2, p: (i, 0)),
-        ),
-        compiler_params=pltpu.CompilerParams(vmem_limit_bytes=40 * 2**20),
-        cost_estimate=pl.CostEstimate(
-            flops=6 * rows * depth * half,
-            bytes_accessed=4 * rows * depth + 6 * depth * half,
-            transcendentals=0,
-        ),
-        name="lower_partial",
-    )(
-        loc1, in1, loc2, in2, jnp.reshape(part, (1,)).astype(jnp.int32),
-        *([ancestor] * (2 * listed)), both, linked, both,
-    )
+            in_specs=specs + [ANY] * len(first),
+            out_specs=(pl.BlockSpec((tile, width), lambda i, l1, l2, at: (i, 0)),) * 2,
+            scratch_shapes=[
+                pltpu.VMEM((listed * BLK, width), BF16),
+                pltpu.VMEM((tile, 2 * width), F32),
+            ],
+        ),
+        compiler_params=pltpu.CompilerParams(vmem_limit_bytes=56 * 2**20),
+        cost_estimate=FREE,
+        name="lower_slots",
+    )(list1, list2, at, *([ancestor] * (2 * listed)), panels, panels, link, *first)
 
 
 def strip_body(strip, w_ref, a_ref, *refs):
@@ -230,7 +247,8 @@
     inner = 4 if strips % 4 == 0 else 1
     if inner == 1:
         whole = strip_product(ancestor, placed, 0, 1)
-        return lax.psum_scatter(whole.astype(F32), "rows", scatter_dimension=1, tiled=True)
+        whole = whole.astype(F32)
+        return lax.psum_scatter(whole, "rows", scatter_dimension=1, tiled=True), []
     depth = strips // inner
     core, side, level = row_at % 2, (row_at // 2) % 2, row_at // 4
     to_core = [(i, i ^ 1) for i in range(strips)]
@@ -242,7 +260,7 @@
     def strip_of(target, x, c):
         return (target * 2 + x) * 2 + c
 
-    layer = []
+    layer, marks = [], []
     for turn in range(depth):
         target = order_table[level, turn]
         far = strip_product(ancestor, placed, strip_of(target, 1 - side, 1 - core), strips)
@@ -250,6 +268,7 @@
         near = strip_product(ancestor, placed, strip_of(target, side, 1 - core), strips)
         near = lax.ppermute(near, "rows", to_core)
         far = strip_product(ancestor, placed, strip_of(target, 1 - side, core), strips, far)
+        marks.append(far)
         far = lax.ppermute(far, "rows", to_side)
         layer.append(
             strip_product(ancestor, placed, strip_of(target, side, core), strips, near, far)
@@ -281,7 +300,7 @@
     for way in (1, -1):
         if arrived[way] is not None:
             total = total + arrived[way].astype(F32)
-    return total
+    return total, marks[:2]
 
 
 def body(
@@ -317,30 +336,25 @@
         beside, link_beside, list_beside, blocks_beside,
         row_at * tile_rows, tile_rows,
     )
-    upper = upper_sums(ancestor, placed)
+    upper, marks = upper_sums(ancestor, placed)
     new_upper = upper[:width].T.astype(BF16)
     next_upper = upper[width:].T.astype(BF16)
 
-    depth = below.shape[0] // 2
-    linked = mm(below[:depth], link_below).astype(BF16)
-    lower_total = None
-    sums_total = None
-    for shift in reversed(range(cols)):
-        part = (col_at + shift) % cols
-        piece = lower_partial(
-            ancestor, below, linked, list_below, blocks_below,
-            col_at * (tile_cols // BLK), part, cols,
-        )
-        sums = jnp.concatenate(
+    given, kept = lower_slots(
+        ancestor, below, link_below, list_below, blocks_below,
+        col_at * (tile_cols // BLK), col_at, marks,
+    )
+
+    def small_sums(piece):
+        return jnp.concatenate(
             [mm(placed[:width], piece), mm(placed[width:], piece[:, half:])], axis=1
         )
-        if shift:
-            pairs = [(i, (i + shift) % cols) for i in range(cols)]
-            piece = lax.ppermute(piece, "cols", pairs)
-            sums = lax.ppermute(sums, "cols", pairs)
-        piece = piece.astype(F32)
-        lower_total = piece if lower_total is None else lower_total + piece
-        sums_total = sums if sums_total is None else sums_total + sums
+
+    def other_column(value):
+        return lax.ppermute(value, "cols", [(i, i ^ 1) for i in range(cols)])
+
+    sums_total = small_sums(kept) + other_column(small_sums(given).astype(BF16)).astype(F32)
+    lower_total = kept.astype(F32) + other_column(given).astype(F32)
     new_lower = lower_total[:, :half].astype(BF16)
     next_lower = lower_total[:, half:].astype(BF16)
 

time: 383 us -> 389 us (1.016)
  waiting for transfers between devices: 162 us -> 178 us
  starting transfers between devices: 30.4 us -> 22.8 us
  Pallas kernels: 112 us -> 107 us
  local copies, waits for them, and re-layouts: 14.8 us -> 18.7 us
    ppermute x4, waiting for transfers between devices: 10.6 us -> 35.2 us  [upper_sums(): far = lax.ppermute(far, 'rows', to_side)]
    all_gather x2, waiting for transfers between devices: 82.5 us -> 62.6 us  [gather_pair(): return lax.all_gather(mine, ('cols', 'rows'), axis=0, tiled=True)]
    ppermute x2, waiting for transfers between devices: 15.1 us -> 30.8 us  [other_column(): return lax.ppermute(value, 'cols', [(i, i ^ 1) for i in range(cols)])]
    ppermute x6, starting transfers between devices: 20 us -> 14.3 us  [upper_sums(): arrived[way] = lax.ppermute(value, 'rows', pairs)]
    ppermute x6, waiting for transfers between devices: 4.18 us -> 0.02 us  [upper_sums(): arrived[way] = lax.ppermute(value, 'rows', pairs)]
    unnamed x55 -> x73, local copies, waits for them, and re-layouts: 10.8 us -> 14.7 us
    pallas_call x2 -> x1, Pallas kernels: 24.3 us -> 20.5 us  [lower_slots(): pl.pallas_call(functools.partial(lower_slots_body, listed // SLOTS, block...]
    dot_general x10 -> x9, matrix products: 15.9 us -> 13.6 us  [mm(): return jnp.dot(left, right, preferred_element_type=F32)]
  transfers between devices with their start and end apart: 23 -> 23, of which waited for: 7 -> 5; matrix products, arithmetic and copies ran while one was open for 10% -> 10% of each run, Pallas kernels for 29% -> 28%
where the time goes in v2:
time: 389 us; the launch traced here: 388 us
  waiting for transfers between devices  178 us (46%)
  Pallas kernels  107 us (28%)
  starting transfers between devices  22.8 us (6%)
  local copies, waits for them, and re-layouts  18.7 us (5%)
  matrix products  18.3 us (5%)
  other arithmetic  17.6 us (5%)
  between operations  17 us (4%)
  blocking collectives  7.72 us (2%)
    pallas_call x16, Pallas kernels, strip_product(): pl.pallas_call(strip_body, out_shape=jax.ShapeDtypeStruct((height, strip_...  82.1 us
    all_gather x2, waiting for transfers between devices, gather_pair(): return lax.all_gather(mine, ('cols', 'rows'), axis=0, tiled=True)  62.6 us
    psum x1, waiting for transfers between devices, body(): sums = lax.psum(sums_total, 'rows')  49.6 us
    ppermute x4, waiting for transfers between devices, upper_sums(): far = lax.ppermute(far, 'rows', to_side)  35.2 us
    ppermute x2, waiting for transfers between devices, other_column(): return lax.ppermute(value, 'cols', [(i, i ^ 1) for i in range(cols)])  30.8 us
    pallas_call x1, Pallas kernels, lower_slots(): pl.pallas_call(functools.partial(lower_slots_body, listed // SLOTS, block...  20.5 us
    unnamed x73, local copies, waits for them, and re-layouts  14.7 us
    ppermute x6, starting transfers between devices, upper_sums(): arrived[way] = lax.ppermute(value, 'rows', pairs)  14.3 us
  transfers between devices with their start and end apart: 23, of which 5 were waited for; matrix products, arithmetic and copies ran while one was open for 10% of the time, Pallas kernels for 28%

profile of v2, /device:TPU:0, one launch (start us, length us, event | category | flops | bytes accessed | tf_op | source)
XLA Modules:
  0.0 387.9 jit_solution(15857745579951780280)
XLA Ops:
  13.7 62.6 %all-gather.5.cloned.1.call-done.u1_ref.u2_ref = bf16[4096,512]{1,0:T(8,128)(2,1)} async-done(((bf16[128,512]{1,0:T(8,128)(2,1)}), bf16[4096,512]{1,0:T(8,128)(2,1)}) %all-gather.5.cloned.1.call-update) | async-done | bytes 4194320 | tf_op jit(solution)/shard_map/all_gather | solution.py:41
  79.5 4.7 %place_panels.1.w_ref = bf16[1024,1536]{1,0:T(8,128)(2,1)S(1)} custom-call(s32[12]{0:T(128)S(1)} %get-tuple-element.28.pos1, s32[12]{0:T(128)S(1)} %convert_element_type.100.in1, s32[12]{0:T(128)S(1)} %get-tuple-element.27.pos2, s32[12]{0:T(128)S(1)} %convert_element_type.101.in2, bf16[4096,512]{1,0:T(8,128)(2,1)S(1)} %copy-done.2, ...), custom_call_target="tpu_custom_call" | custom-call | flops 805306368 | bytes 6291456 | tf_op jit(solution)/shard_map/place_panels/pallas_call | solution.py:92
  84.3 5.3 %strip_product.16 = bf16[1024,768]{1,0:T(8,128)(2,1)} custom-call(s32[1]{0:T(128)} %bitcast.4.strip, bf16[1024,1536]{1,0:T(8,128)(2,1)S(1)} %place_panels.1.w_ref, bf16[1536,12288]{1,0:T(8,128)(2,1)} %a_ref.31), custom_call_target="tpu_custom_call" | custom-call | flops 2415919104 | bytes 7077888 | tf_op jit(solution)/shard_map/strip_product/pallas_call | solution.py:216
  90.5 5.3 %strip_product.18 = bf16[1024,768]{1,0:T(8,128)(2,1)} custom-call(s32[1]{0:T(128)} %bitcast.7.strip, bf16[1024,1536]{1,0:T(8,128)(2,1)S(1)} %place_panels.1.w_ref, bf16[1536,12288]{1,0:T(8,128)(2,1)} %a_ref.31), custom_call_target="tpu_custom_call" | custom-call | flops 2415919104 | bytes 7077888 | tf_op jit(solution)/shard_map/strip_product/pallas_call | solution.py:216
  96.0 5.3 %strip_product.28 = bf16[1024,768]{1,0:T(8,128)(2,1)} custom-call(s32[1]{0:T(128)} %bitcast.19.strip, bf16[1024,1536]{1,0:T(8,128)(2,1)S(1)} %place_panels.1.w_ref, bf16[1536,12288]{1,0:T(8,128)(2,1)} %a_ref.31), custom_call_target="tpu_custom_call" | custom-call | flops 2415919104 | bytes 7077888 | tf_op jit(solution)/shard_map/strip_product/pallas_call | solution.py:216
  101.5 5.7 %strip_product.17.refs_35_ = bf16[1024,768]{1,0:T(8,128)(2,1)} custom-call(s32[1]{0:T(128)} %bitcast.3.strip, bf16[1024,1536]{1,0:T(8,128)(2,1)S(1)} %place_panels.1.w_ref, bf16[1536,12288]{1,0:T(8,128)(2,1)} %a_ref.31, bf16[1024,768]{1,0:T(8,128)(2,1)} %collective-permute-done.refs_0_), custom_call_target="tpu_custom_call" | custom-call | flops 2415919104 | bytes 8650752 | tf_op jit(solution)/shard_map/strip_product/pallas_call | solution.py:216
  113.2 5.3 %strip_product.30 = bf16[1024,768]{1,0:T(8,128)(2,1)} custom-call(s32[1]{0:T(128)} %bitcast.21.strip, bf16[1024,1536]{1,0:T(8,128)(2,1)S(1)} %place_panels.1.w_ref, bf16[1536,12288]{1,0:T(8,128)(2,1)} %a_ref.31), custom_call_target="tpu_custom_call" | custom-call | flops 2415919104 | bytes 7077888 | tf_op jit(solution)/shard_map/strip_product/pallas_call | solution.py:216
  118.5 5.6 %strip_product.25 = bf16[1024,768]{1,0:T(8,128)(2,1)} custom-call(s32[1]{0:T(128)} %bitcast.17.strip, bf16[1024,1536]{1,0:T(8,128)(2,1)S(1)} %place_panels.1.w_ref, bf16[1536,12288]{1,0:T(8,128)(2,1)} %a_ref.31), custom_call_target="tpu_custom_call" | custom-call | flops 2415919104 | bytes 7077888 | tf_op jit(solution)/shard_map/strip_product/pallas_call | solution.py:216
  129.0 5.6 %strip_product.19.refs_36_ = bf16[1024,768]{1,0:T(8,128)(2,1)} custom-call(s32[1]{0:T(128)} %bitcast.6.strip, bf16[1024,1536]{1,0:T(8,128)(2,1)S(1)} %place_panels.1.w_ref, bf16[1536,12288]{1,0:T(8,128)(2,1)} %a_ref.31, bf16[1024,768]{1,0:T(8,128)(2,1)} %collective-permute-done.1.refs_0_), custom_call_target="tpu_custom_call" | custom-call | flops 2415919104 | bytes 8650752 | tf_op jit(solution)/shard_map/strip_product/pallas_call | solution.py:216
  139.5 12.8 %collective-permute-done.10.refs_1_ = bf16[1024,768]{1,0:T(8,128)(2,1)} collective-permute-done((bf16[1024,768]{1,0:T(8,128)(2,1)}, bf16[1024,768]{1,0:T(8,128)(2,1)}, u32[]{:S(2)}, u32[]{:S(2)}) %collective-permute-start.10) | collective-permute-done | bytes 1572896 | tf_op jit(solution)/shard_map/ppermute | solution.py:272
  152.4 5.9 %strip_product.29 = bf16[1024,768]{1,0:T(8,128)(2,1)} custom-call(s32[1]{0:T(128)} %bitcast.18.strip, bf16[1024,1536]{1,0:T(8,128)(2,1)S(1)} %place_panels.1.w_ref, bf16[1536,12288]{1,0:T(8,128)(2,1)} %a_ref.31, bf16[1024,768]{1,0:T(8,128)(2,1)} %collective-permute-done.9.refs_0_, bf16[1024,768]{1,0:T(8,128)(2,1)} %collective-permute-done.10.refs_1_), custom_call_target="tpu_custom_call" | custom-call | flops 2415919104 | bytes 10223616 | tf_op jit(solution)/shard_map/strip_product/pallas_call | solution.py:216
  158.3 4.5 %collective-permute-start.13 = (bf16[1024,768]{1,0:T(8,128)(2,1)}, bf16[1024,768]{1,0:T(8,128)(2,1)}, u32[]{:S(2)}, u32[]{:S(2)}) collective-permute-start(bf16[1024,768]{1,0:T(8,128)(2,1)} %strip_product.29), channel_id=1, source_target_pairs={{0,8},{2,10},{4,12},{6,14},{1,9},{3,11},{5,13},{7,15}} | collective-permute-start | bytes 4718600 | tf_op jit(solution)/shard_map/ppermute | solution.py:298
  170.1 5.3 %strip_product.20 = bf16[1024,768]{1,0:T(8,128)(2,1)} custom-call(s32[1]{0:T(128)} %bitcast.10.strip, bf16[1024,1536]{1,0:T(8,128)(2,1)S(1)} %place_panels.1.w_ref, bf16[1536,12288]{1,0:T(8,128)(2,1)} %a_ref.31), custom_call_target="tpu_custom_call" | custom-call | flops 2415919104 | bytes 7077888 | tf_op jit(solution)/shard_map/strip_product/pallas_call | solution.py:216
  175.4 20.5 %lower_slots.1 = (bf16[1536,512]{1,0:T(8,128)(2,1)}, bf16[1536,512]{1,0:T(8,128)(2,1)}) custom-call(s32[16]{0:T(128)} %l1.1, s32[16]{0:T(128)} %l2.1, s32[2]{0:T(128)} %pad_add_fusion.at, bf16[1536,12288]{1,0:T(8,128)(2,1)} %a_ref.31, bf16[1536,12288]{1,0:T(8,128)(2,1)} %a_ref.31, bf16[1536,12288]{1,0:T(8,128)(2,1)} %a_ref.31, bf16[1536,12288]{1,0:T(8,128)(2,1)} %a_ref.31, ...), custom_call_target="tpu_custom_call" | custom-call | tf_op jit(solution)/shard_map/lower_slots/pallas_call | solution.py:177
  198.4 4.6 %strip_product.26 = bf16[1024,768]{1,0:T(8,128)(2,1)S(1)} custom-call(s32[1]{0:T(128)} %bitcast.16.strip, bf16[1024,1536]{1,0:T(8,128)(2,1)S(1)} %place_panels.1.w_ref, bf16[1536,12288]{1,0:T(8,128)(2,1)} %a_ref.31, bf16[1024,768]{1,0:T(8,128)(2,1)} %collective-permute-done.7.refs_0_), custom_call_target="tpu_custom_call" | custom-call | flops 2415919104 | bytes 8650752 | tf_op jit(solution)/shard_map/strip_product/pallas_call | solution.py:216
  208.3 5.0 %strip_product.31 = bf16[1024,768]{1,0:T(8,128)(2,1)S(1)} custom-call(s32[1]{0:T(128)} %bitcast.20.strip, bf16[1024,1536]{1,0:T(8,128)(2,1)S(1)} %place_panels.1.w_ref, bf16[1536,12288]{1,0:T(8,128)(2,1)} %a_ref.31, bf16[1024,768]{1,0:T(8,128)(2,1)} %collective-permute-done.11.refs_0_, bf16[1024,768]{1,0:T(8,128)(2,1)} %collective-permute-done.12.refs_1_), custom_call_target="tpu_custom_call" | custom-call | flops 2415919104 | bytes 10223616 | tf_op jit(solution)/shard_map/strip_product/pallas_call | solution.py:216
  214.6 4.9 %add_convert_fusion.4 = (bf16[1024,768]{1,0:T(8,128)(2,1)}, bf16[1024,768]{1,0:T(8,128)(2,1)}) fusion(bf16[1024,768]{1,0:T(8,128)(2,1)} %collective-permute-done.13, bf16[1024,768]{1,0:T(8,128)(2,1)} %strip_product.29, bf16[1024,768]{1,0:T(8,128)(2,1)S(1)} %strip_product.31, pred[]{:T(512)S(6)} %eq.47, bf16[1024,768]{1,0:T(8,128)(2,1)} %collective-permute-done.16, ...), kind=kLoop, calls=%fused_computation.4 | loop fusion | flops 7864320 | bytes 9437186 | tf_op jit(solution)/shard_map/convert_element_type | solution.py:241
  223.8 5.3 %strip_product.22 = bf16[1024,768]{1,0:T(8,128)(2,1)} custom-call(s32[1]{0:T(128)} %bitcast.11.strip, bf16[1024,1536]{1,0:T(8,128)(2,1)S(1)} %place_panels.1.w_ref, bf16[1536,12288]{1,0:T(8,128)(2,1)} %a_ref.31, bf16[1024,768]{1,0:T(8,128)(2,1)S(1)} %collective-permute-done.4.refs_0_), custom_call_target="tpu_custom_call" | custom-call | flops 2415919104 | bytes 8650752 | tf_op jit(solution)/shard_map/strip_product/pallas_call | solution.py:216
  230.2 30.8 %collective-permute-done.19 = bf16[512,768]{0,1:T(8,128)(2,1)S(1)} collective-permute-done((bf16[512,768]{0,1:T(8,128)(2,1)S(1)}, bf16[512,768]{0,1:T(8,128)(2,1)S(1)}, u32[]{:S(2)}, u32[]{:S(2)}) %collective-permute-start.19) | collective-permute-done | bytes 786464 | tf_op jit(solution)/shard_map/ppermute | solution.py:354
  274.4 4.5 %add_convert_fusion.3 = (bf16[1024,768]{1,0:T(8,128)(2,1)}, bf16[1024,768]{1,0:T(8,128)(2,1)}) fusion(bf16[1024,768]{1,0:T(8,128)(2,1)} %collective-permute-done.14, bf16[1024,768]{1,0:T(8,128)(2,1)S(1)} %strip_product.27, bf16[1024,768]{1,0:T(8,128)(2,1)} %collective-permute-done.17, bf16[1024,768]{1,0:T(8,128)(2,1)S(1)} %copy-done.4, pred[]{:T(512)S(6)} %eq.48), kind=kLoop, calls=%fused_computation.3 | loop fusion | flops 7077888 | bytes 9437185 | tf_op jit(solution)/shard_map/convert_element_type | solution.py:241
  282.6 22.4 %collective-permute-done.5.refs_1_ = bf16[1024,768]{1,0:T(8,128)(2,1)} collective-permute-done((bf16[1024,768]{1,0:T(8,128)(2,1)}, bf16[1024,768]{1,0:T(8,128)(2,1)}, u32[]{:S(2)}, u32[]{:S(2)}) %collective-permute-start.5) | collective-permute-done | bytes 1572896 | tf_op jit(solution)/shard_map/ppermute | solution.py:272
  305.0 5.0 %strip_product.23 = bf16[1024,768]{1,0:T(8,128)(2,1)S(1)} custom-call(s32[1]{0:T(128)} %bitcast.9.strip, bf16[1024,1536]{1,0:T(8,128)(2,1)S(1)} %place_panels.1.w_ref, bf16[1536,12288]{1,0:T(8,128)(2,1)} %a_ref.31, bf16[1024,768]{1,0:T(8,128)(2,1)} %collective-permute-done.3.refs_0_, bf16[1024,768]{1,0:T(8,128)(2,1)} %collective-permute-done.5.refs_1_), custom_call_target="tpu_custom_call" | custom-call | flops 2415919104 | bytes 10223616 | tf_op jit(solution)/shard_map/strip_product/pallas_call | solution.py:216
  312.4 49.6 %all-reduce.2.cloned.1.call-done = f32[512,768]{0,1:T(8,128)} async-done(((f32[512,768]{0,1:T(8,128)}), f32[512,768]{0,1:T(8,128)}) %all-reduce.2.cloned.1.call-update) | async-done | bytes 1572880 | tf_op jit(solution)/shard_map/psum | solution.py:361
  363.2 7.7 %all_gather.11 = bf16[512,512]{0,1:T(8,128)(2,1)S(1)} all-gather(bf16[512,256]{0,1:T(8,128)(2,1)S(1)} %fusion.19), channel_id=1, replica_groups=mesh['rows'=16,'cols'=2] {'cols'}, dimensions={1}, use_global_device_ids=true | all-gather | bytes 786432 | tf_op jit(solution)/shard_map/all_gather | solution.py:370
  (146 shorter events, 76.6 us)
Async XLA Ops:
  7.2 69.0 %all-gather.5.cloned.1.call-start = ((), (), s32[]{:S(2)}) async-start(), calls=%async_computation.1 | async-start | bytes 4325376 | tf_op jit(solution)/shard_map/all_gather | solution.py:41
  9.6 165.8 %all-gather.3.cloned.1.call-start = ((), (), s32[]{:S(2)}) async-start(), calls=%async_computation | async-start | bytes 4325376 | tf_op jit(solution)/shard_map/all_gather | solution.py:41
  10.6 351.4 %all-reduce.2.cloned.1.call-start = ((), (), s32[]{:S(2)}) async-start(), calls=%async_computation.2 | async-start | bytes 3145728 | tf_op jit(solution)/shard_map/psum | solution.py:361
  89.5 12.0 %collective-permute-start = (bf16[1024,768]{1,0:T(8,128)(2,1)}, bf16[1024,768]{1,0:T(8,128)(2,1)}, u32[]{:S(2)}, u32[]{:S(2)}) collective-permute-start(bf16[1024,768]{1,0:T(8,128)(2,1)} %strip_product.16), channel_id=1, source_target_pairs={{0,2},{2,0},{4,6},{6,4},{8,10},{10,8},{12,14},{14,12},{16,18},{18,... | collective-permute-start | bytes 4718600 | tf_op jit(solution)/shard_map/ppermute | solution.py:267
  95.8 33.3 %collective-permute-start.1 = (bf16[1024,768]{1,0:T(8,128)(2,1)}, bf16[1024,768]{1,0:T(8,128)(2,1)}, u32[]{:S(2)}, u32[]{:S(2)}) collective-permute-start(bf16[1024,768]{1,0:T(8,128)(2,1)} %strip_product.18), channel_id=1, source_target_pairs={{0,2},{2,0},{4,6},{6,4},{8,10},{10,8},{12,14},{14,12},{16,18},{18,... | collective-permute-start | bytes 4718600 | tf_op jit(solution)/shard_map/ppermute | solution.py:267
  101.3 38.3 %collective-permute-start.9 = (bf16[1024,768]{1,0:T(8,128)(2,1)}, bf16[1024,768]{1,0:T(8,128)(2,1)}, u32[]{:S(2)}, u32[]{:S(2)}) collective-permute-start(bf16[1024,768]{1,0:T(8,128)(2,1)} %strip_product.28), channel_id=1, source_target_pairs={{0,2},{2,0},{4,6},{6,4},{8,10},{10,8},{12,14},{14,12},{16,18},{18,... | collective-permute-start | bytes 4718600 | tf_op jit(solution)/shard_map/ppermute | solution.py:269
  107.3 45.1 %collective-permute-start.10 = (bf16[1024,768]{1,0:T(8,128)(2,1)}, bf16[1024,768]{1,0:T(8,128)(2,1)}, u32[]{:S(2)}, u32[]{:S(2)}) collective-permute-start(bf16[1024,768]{1,0:T(8,128)(2,1)} %strip_product.17.refs_35_), channel_id=1, source_target_pairs={{0,4},{2,6},{4,0},{6,2},{8,12},{10,14},{12,8},{14,10},{16,20},{18,... | collective-permute-start | bytes 4718600 | tf_op jit(solution)/shard_map/ppermute | solution.py:272
  118.5 79.3 %collective-permute-start.11 = (bf16[1024,768]{1,0:T(8,128)(2,1)}, bf16[1024,768]{1,0:T(8,128)(2,1)}, u32[]{:S(2)}, u32[]{:S(2)}) collective-permute-start(bf16[1024,768]{1,0:T(8,128)(2,1)} %strip_product.30), channel_id=1, source_target_pairs={{0,2},{2,0},{4,6},{6,4},{8,10},{10,8},{12,14},{14,12},{16,18},{18,... | collective-permute-start | bytes 4718600 | tf_op jit(solution)/shard_map/ppermute | solution.py:269
  124.1 73.8 %collective-permute-start.7 = (bf16[1024,768]{1,0:T(8,128)(2,1)}, bf16[1024,768]{1,0:T(8,128)(2,1)}, u32[]{:S(2)}, u32[]{:S(2)}) collective-permute-start(bf16[1024,768]{1,0:T(8,128)(2,1)} %strip_product.25), channel_id=1, source_target_pairs={{0,2},{2,0},{4,6},{6,4},{8,10},{10,8},{12,14},{14,12},{16,18},{18,... | collective-permute-start | bytes 4718600 | tf_op jit(solution)/shard_map/ppermute | solution.py:267
  134.6 70.8 %collective-permute-start.12 = (bf16[1024,768]{1,0:T(8,128)(2,1)}, bf16[1024,768]{1,0:T(8,128)(2,1)}, u32[]{:S(2)}, u32[]{:S(2)}) collective-permute-start(bf16[1024,768]{1,0:T(8,128)(2,1)} %strip_product.19.refs_36_), channel_id=1, source_target_pairs={{0,4},{2,6},{4,0},{6,2},{8,12},{10,14},{12,8},{14,10},{16,20},{18,... | collective-permute-start | bytes 4718600 | tf_op jit(solution)/shard_map/ppermute | solution.py:272
  158.3 49.2 %collective-permute-start.13 = (bf16[1024,768]{1,0:T(8,128)(2,1)}, bf16[1024,768]{1,0:T(8,128)(2,1)}, u32[]{:S(2)}, u32[]{:S(2)}) collective-permute-start(bf16[1024,768]{1,0:T(8,128)(2,1)} %strip_product.29), channel_id=1, source_target_pairs={{0,8},{2,10},{4,12},{6,14},{1,9},{3,11},{5,13},{7,15}} | collective-permute-start | bytes 4718600 | tf_op jit(solution)/shard_map/ppermute | solution.py:298
  168.2 45.1 %collective-permute-start.16 = (bf16[1024,768]{1,0:T(8,128)(2,1)}, bf16[1024,768]{1,0:T(8,128)(2,1)}, u32[]{:S(2)}, u32[]{:S(2)}) collective-permute-start(bf16[1024,768]{1,0:T(8,128)(2,1)} %strip_product.29), channel_id=1, source_target_pairs={{24,16},{26,18},{28,20},{30,22},{25,17},{27,19},{29,21},{31,23}} | collective-permute-start | bytes 4718600 | tf_op jit(solution)/shard_map/ppermute | solution.py:298
  197.8 21.8 %collective-permute-start.6 = (bf16[1024,768]{1,0:T(8,128)(2,1)S(1)}, bf16[1024,768]{1,0:T(8,128)(2,1)S(1)}, u32[]{:S(2)}, u32[]{:S(2)}) collective-permute-start(bf16[1024,768]{1,0:T(8,128)(2,1)S(1)} %copy-done.12), channel_id=1, source_target_pairs={{0,2},{2,0},{4,6},{6,4},{8,10},{10,8},{12,14},{14,12},{16,18},{18,... | collective-permute-start | bytes 4718600 | tf_op jit(solution)/shard_map/ppermute | solution.py:269
  198.0 24.1 %collective-permute-start.4 = (bf16[1024,768]{1,0:T(8,128)(2,1)S(1)}, bf16[1024,768]{1,0:T(8,128)(2,1)S(1)}, u32[]{:S(2)}, u32[]{:S(2)}) collective-permute-start(bf16[1024,768]{1,0:T(8,128)(2,1)S(1)} %copy-done.14), channel_id=1, source_target_pairs={{0,2},{2,0},{4,6},{6,4},{8,10},{10,8},{12,14},{14,12},{16,18},{18,... | collective-permute-start | bytes 4718600 | tf_op jit(solution)/shard_map/ppermute | solution.py:267
  205.4 55.6 %collective-permute-start.8 = (bf16[1024,768]{1,0:T(8,128)(2,1)S(1)}, bf16[1024,768]{1,0:T(8,128)(2,1)S(1)}, u32[]{:S(2)}, u32[]{:S(2)}) collective-permute-start(bf16[1024,768]{1,0:T(8,128)(2,1)S(1)} %strip_product.26), channel_id=1, source_target_pairs={{0,4},{2,6},{4,0},{6,2},{8,12},{10,14},{12,8},{14,10},{16,20},{18,... | collective-permute-start | bytes 4718600 | tf_op jit(solution)/shard_map/ppermute | solution.py:272
  207.5 64.8 %collective-permute-start.2 = (bf16[1536,512]{1,0:T(8,128)(2,1)}, bf16[1536,512]{1,0:T(8,128)(2,1)}, u32[]{:S(2)}, u32[]{:S(2)}) collective-permute-start(bf16[1536,512]{1,0:T(8,128)(2,1)} %get-tuple-element.10), channel_id=1, source_target_pairs={{0,1},{1,0},{2,3},{3,2},{4,5},{5,4},{6,7},{7,6},{8,9},{9,8},{10,11... | collective-permute-start | bytes 4718600 | tf_op jit(solution)/shard_map/ppermute | solution.py:354
  213.3 47.7 %collective-permute-start.19 = (bf16[512,768]{0,1:T(8,128)(2,1)S(1)}, bf16[512,768]{0,1:T(8,128)(2,1)S(1)}, u32[]{:S(2)}, u32[]{:S(2)}) collective-permute-start(bf16[512,768]{0,1:T(8,128)(2,1)S(1)} %pad_maximum_fusion), channel_id=1, source_target_pairs={{0,1},{1,0},{2,3},{3,2},{4,5},{5,4},{6,7},{7,6},{8,9},{9,8},{10,11... | collective-permute-start | bytes 2359304 | tf_op jit(solution)/shard_map/ppermute | solution.py:354
  219.6 54.8 %collective-permute-start.14 = (bf16[1024,768]{1,0:T(8,128)(2,1)}, bf16[1024,768]{1,0:T(8,128)(2,1)}, u32[]{:S(2)}, u32[]{:S(2)}) collective-permute-start(bf16[1024,768]{1,0:T(8,128)(2,1)} %get-tuple-element.29), channel_id=1, source_target_pairs={{0,8},{2,10},{4,12},{6,14},{8,16},{10,18},{12,20},{14,22},{1,9},{3... | collective-permute-start | bytes 4718600 | tf_op jit(solution)/shard_map/ppermute | solution.py:298
  222.0 52.3 %collective-permute-start.17 = (bf16[1024,768]{1,0:T(8,128)(2,1)}, bf16[1024,768]{1,0:T(8,128)(2,1)}, u32[]{:S(2)}, u32[]{:S(2)}) collective-permute-start(bf16[1024,768]{1,0:T(8,128)(2,1)} %get-tuple-element.30), channel_id=1, source_target_pairs={{16,8},{18,10},{20,12},{22,14},{24,16},{26,18},{28,20},{30,22},{17... | collective-permute-start | bytes 4718600 | tf_op jit(solution)/shard_map/ppermute | solution.py:298
  261.0 21.6 %collective-permute-start.3 = (bf16[1024,768]{1,0:T(8,128)(2,1)}, bf16[1024,768]{1,0:T(8,128)(2,1)}, u32[]{:S(2)}, u32[]{:S(2)}) collective-permute-start(bf16[1024,768]{1,0:T(8,128)(2,1)} %strip_product.20), channel_id=1, source_target_pairs={{0,2},{2,0},{4,6},{6,4},{8,10},{10,8},{12,14},{14,12},{16,18},{18,... | collective-permute-start | bytes 4718600 | tf_op jit(solution)/shard_map/ppermute | solution.py:269
  262.2 42.7 %collective-permute-start.5 = (bf16[1024,768]{1,0:T(8,128)(2,1)}, bf16[1024,768]{1,0:T(8,128)(2,1)}, u32[]{:S(2)}, u32[]{:S(2)}) collective-permute-start(bf16[1024,768]{1,0:T(8,128)(2,1)} %strip_product.22), channel_id=1, source_target_pairs={{0,4},{2,6},{4,0},{6,2},{8,12},{10,14},{12,8},{14,10},{16,20},{18,... | collective-permute-start | bytes 4718600 | tf_op jit(solution)/shard_map/ppermute | solution.py:272
  278.9 97.6 %collective-permute-start.15 = (bf16[1024,768]{1,0:T(8,128)(2,1)}, bf16[1024,768]{1,0:T(8,128)(2,1)}, u32[]{:S(2)}, u32[]{:S(2)}) collective-permute-start(bf16[1024,768]{1,0:T(8,128)(2,1)} %get-tuple-element.35), channel_id=1, source_target_pairs={{0,8},{2,10},{4,12},{6,14},{8,16},{10,18},{12,20},{14,22},{16,24},... | collective-permute-start | bytes 4718600 | tf_op jit(solution)/shard_map/ppermute | solution.py:298
  281.3 95.1 %collective-permute-start.18 = (bf16[1024,768]{1,0:T(8,128)(2,1)}, bf16[1024,768]{1,0:T(8,128)(2,1)}, u32[]{:S(2)}, u32[]{:S(2)}) collective-permute-start(bf16[1024,768]{1,0:T(8,128)(2,1)} %get-tuple-element.36), channel_id=1, source_target_pairs={{8,0},{10,2},{12,4},{14,6},{16,8},{18,10},{20,12},{22,14},{24,16},... | collective-permute-start | bytes 4718600 | tf_op jit(solution)/shard_map/ppermute | solution.py:298
  312.4 59.6 %copy-start.19 = (f32[512,256]{0,1:T(8,128)S(1)}, f32[512,256]{0,1:T(8,128)}, u32[]{:S(2)}) copy-start(f32[512,256]{0,1:T(8,128)} %fusion.25) | copy-start | bytes 1572868
  (33 other events, 238.8 us)
Sparse Core Ops, SparseCore 0:
  11.5 64.7 all-gather.4
  79.7 68.0 all-gather.2
  265.1 96.8 all-reduce.1
